TPU v7x, 32 devices: a whole 2x2x4 slice. The times are simulated.
32 devices in a mesh: grid: 8 (over z, y), space: 4 (over x, core).
Axes of the slice: x: 2, y: 2, z: 4, core: 2. Of those that a mesh axis runs over, the one named last changes fastest.
Arguments:
- density: float32 [8, 512, 64, 128], P('grid', 'space'), may hold values from -6 to 6
- kappa: float32 [8, 512, 64, 128], P('grid', 'space'), may hold values from 0.02 to 0.16
- levels: int32 [8, 3], P('grid'), may hold values from 3 to 6, as said below
- coefs: int32 [8], P('grid'), may hold values from -2 to 1, as said below
Outputs:
- combined: float32 [8, 512, 64, 128], P('grid', 'space')
Inputs may be any that keep to these rules, and one draw needn't show every extreme that they name: `levels`: each level vector is (3, 3, 3) plus nonnegative integers summing to 1, 2 or 3, no two grids alike; a level at or above log2 of an axis's cells keeps that whole axis. coefs[g] is +1 where the grid's levels sum to 12 or 10 and -2 where they sum to 11.
All inputs are finite; a program needn't handle non-finite values.
Results may differ from a plain program's by a relative error of at most 0.0003.
Values sent between devices are 32-bit elements; how exact they have to be, the bound alone decides.
A program may use at most 128 MiB of HBM per device.

v0:
```python
import jax
import jax.numpy as jnp
import numpy as np
from jax import lax
from jax.sharding import PartitionSpec as P

ITERS = 8


def extended_2(value, sides, width):
    for axis, dim in sides:
        devices, length = (lax.axis_size(axis), value.shape[dim])
        up = [(i, (i + 1) % devices) for i in range(devices)]
        down = [(j, i) for i, j in up]
        last = lax.slice_in_dim(value, length - width, length, axis=dim)
        initial = lax.slice_in_dim(value, 0, width, axis=dim)
        before = lax.ppermute(last, axis, up)
        after = lax.ppermute(initial, axis, down)
        value = jnp.concatenate([before, value, after], axis=dim)
    return value


def build_tables(count):
    depth = count.bit_length() - 1
    hier = np.eye(count)
    dehier = np.eye(count)
    level_table = np.zeros(count, dtype=np.int64)
    for index in range(1, count):
        trailing = 0
        while index >> trailing & 1 == 0:
            trailing += 1
        spacing = 1 << trailing
        level_table[index] = depth - trailing
        hier[index, (index - spacing) % count] -= 0.5
        hier[index, (index + spacing) % count] -= 0.5
    for trailing in range(depth - 1, -1, -1):
        spacing = 1 << trailing
        for index in range(spacing, count, 2 * spacing):
            dehier[index] = dehier[index] + 0.5 * (
                dehier[(index - spacing) % count] + dehier[(index + spacing) % count]
            )
    return (
        jnp.asarray(hier, jnp.float32),
        jnp.asarray(dehier, jnp.float32),
        jnp.asarray(level_table.astype(np.int32)),
    )


def slab_tables(rows):
    hier = np.zeros((rows, rows + 1))
    dehier = np.eye(rows + 1)
    for index in range(1, rows):
        trailing = 0
        while index >> trailing & 1 == 0:
            trailing += 1
        spacing = 1 << trailing
        hier[index, index] += 1.0
        hier[index, index - spacing] -= 0.5
        hier[index, index + spacing] -= 0.5
    depth = rows.bit_length() - 1
    for trailing in range(depth - 1, -1, -1):
        spacing = 1 << trailing
        for index in range(spacing, rows, 2 * spacing):
            dehier[index] = dehier[index] + 0.5 * (
                dehier[index - spacing] + dehier[index + spacing]
            )
    return (jnp.asarray(hier, jnp.float32), jnp.asarray(dehier[:rows], jnp.float32))


def along_first(field, matrix):
    return jnp.einsum("wx,xyz->wyz", matrix, field, precision=lax.Precision.HIGHEST)


def along_second(field, matrix):
    return jnp.einsum("vy,xyz->xvz", matrix, field, precision=lax.Precision.HIGHEST)


def along_third(field, matrix):
    return jnp.einsum("xyz,wz->xyw", field, matrix, precision=lax.Precision.HIGHEST)


def padded_field(field):
    return extended_2(field, (("space", 0),), 1)


def local(density, kappa, levels, coefs):
    slab_rows = density.shape[1]
    width_y = density.shape[2]
    width_z = density.shape[3]
    members = lax.axis_size("space")
    position = lax.axis_index("space")
    width_x = slab_rows * members
    hier_x, dehier_x, level_x = build_tables(width_x)
    hier_y, dehier_y, level_y = build_tables(width_y)
    hier_z, dehier_z, level_z = build_tables(width_z)
    coeff = kappa[0]
    field = density[0]
    coeff_pad = extended_2(coeff, (("space", 0),), 1)
    face_xp = 0.5 * (coeff + coeff_pad[2:])
    face_xm = 0.5 * (coeff + coeff_pad[:-2])
    face_yp = 0.5 * (coeff + jnp.roll(coeff, -1, 1))
    face_ym = 0.5 * (coeff + jnp.roll(coeff, 1, 1))
    face_zp = 0.5 * (coeff + jnp.roll(coeff, -1, 2))
    face_zm = 0.5 * (coeff + jnp.roll(coeff, 1, 2))
    for sweep_index in range(ITERS):
        extended = padded_field(field)
        flux = face_xp * (extended[2:] - field) + face_xm * (extended[:-2] - field)
        flux = (
            flux
            + face_yp * (jnp.roll(field, -1, 1) - field)
            + face_ym * (jnp.roll(field, 1, 1) - field)
        )
        flux = (
            flux
            + face_zp * (jnp.roll(field, -1, 2) - field)
            + face_zm * (jnp.roll(field, 1, 2) - field)
        )
        field = field + flux
    level_vec = levels[0]
    weight = coefs[0].astype(jnp.float32)
    mask_x = (level_x <= level_vec[0]).astype(jnp.float32)
    mask_y = (level_y <= level_vec[1]).astype(jnp.float32)
    mask_z = (level_z <= level_vec[2]).astype(jnp.float32)
    surplus = along_third(along_second(field, hier_y), hier_z)
    hier_coarse, dehier_coarse, level_coarse = build_tables(members)
    hier_slab, dehier_slab = slab_tables(slab_rows)
    next_index = (position + 1) % members
    coarse = lax.all_gather(surplus[0:1], "space", axis=0, tiled=True)
    coarse_surplus = along_first(coarse, hier_coarse)
    next_plane = lax.dynamic_slice_in_dim(coarse, next_index, 1)
    fine = along_first(jnp.concatenate([surplus, next_plane], axis=0), hier_slab)
    own_plane = lax.dynamic_slice_in_dim(coarse_surplus, position, 1)
    surplus = jnp.concatenate([own_plane, fine[1:]], axis=0)
    slab_mask_x = lax.dynamic_slice_in_dim(mask_x, position * slab_rows, slab_rows)
    mask = slab_mask_x[:, None, None] * mask_y[None, :, None] * mask_z[None, None, :]
    total = lax.psum(weight * mask * surplus, "grid")
    masked = mask * total
    coarse_total = lax.all_gather(masked[0:1], "space", axis=0, tiled=True)
    coarse_values = along_first(coarse_total, dehier_coarse)
    own_value = lax.dynamic_slice_in_dim(coarse_values, position, 1)
    next_value = lax.dynamic_slice_in_dim(coarse_values, next_index, 1)
    extended = jnp.concatenate([own_value, masked[1:], next_value], axis=0)
    result = along_first(extended, dehier_slab)
    result = along_third(along_second(result, dehier_y), dehier_z)
    return result[None]


def solution(mesh):
    in_specs = (
        P("grid", "space", None, None),
        P("grid", "space", None, None),
        P("grid", None),
        P("grid"),
    )
    out_specs = P("grid", "space", None, None)
    return jax.shard_map(local, mesh=mesh, in_specs=in_specs, out_specs=out_specs, check_vma=False)
```

profile of v0, /device:TPU:0, one launch (start us, length us, event | category | flops | bytes accessed | tf_op | source)
XLA Modules:
  0.0 599.0 jit_solution(16235181673872439282)
XLA Ops:
  12.2 12.9 %fusion.208 = (f32[128,63,128]{2,1,0:T(8,128)}, f32[128,63,128]{2,1,0:T(8,128)}, f32[128,63,128]{2,1,0:T(8,128)}, f32[128,63,128]{2,1,0:T(8,128)}) fusion(f32[128,64,128]{2,1,0:T(8,128)} %bitcast.55, f32[128,64,128]{2,1,0:T(8,128)} %bitcast.67), kind=kLoop, calls=%fused_computation.262 | loop fusion | bytes 33030144 | tf_op jit(solution)/shard_map/jit(_roll_static)/slice | solution.py:101
  25.1 7.1 %fusion.210 = (f32[128,64,127]{2,1,0:T(8,128)}, f32[128,64,127]{2,1,0:T(8,128)}, f32[128,64,127]{2,1,0:T(8,128)}, f32[128,64,127]{2,1,0:T(8,128)}) fusion(f32[128,64,128]{2,1,0:T(8,128)S(1)} %bitcast.57, f32[128,64,128]{2,1,0:T(8,128)S(1)} %bitcast.69), kind=kLoop, calls=%fused_computation.264 | loop fusion | bytes 33292288 | tf_op jit(solution)/shard_map/jit(_roll_static)/slice | solution.py:103
  32.2 7.0 %fusion.211 = (f32[128,64,1]{2,1,0:T(8,128)}, f32[128,64,1]{2,1,0:T(8,128)}, f32[128,64,1]{2,1,0:T(8,128)}, f32[128,64,1]{2,1,0:T(8,128)}) fusion(f32[128,64,128]{2,1,0:T(8,128)S(1)} %bitcast.58, f32[128,64,128]{2,1,0:T(8,128)S(1)} %bitcast.70), kind=kLoop, calls=%fused_computation.265 | loop fusion | bytes 262144 | tf_op jit(solution)/shard_map/jit(_roll_static)/slice | solution.py:103
  44.1 34.7 %fusion.93 = (f32[128,64,128]{2,1,0:T(8,128)S(1)}, f32[128,64,128]{2,1,0:T(8,128)}, f32[128,64,128]{2,1,0:T(8,128)}, f32[128,64,128]{2,1,0:T(8,128)}, f32[128,64,128]{2,1,0:T(8,128)}) fusion(f32[128,64,128]{2,1,0:T(8,128)} %bitcast.68, f32[1,64,128]{2,1,0:T(8,128)S(1)} %collective-permute-done.3, f32[1,64,128]{2,1,0:T(8,128)S(1)} %collective-permute-done.1, ...), kind=kLoop, calls=%fused_computation.108 | loop fusion | flops 44040192 | bytes 67239936 | tf_op jit(solution)/shard_map/add | solution.py:118
  78.8 4.9 fusion.203
  83.7 4.8 fusion.204
  88.4 8.9 %fusion.206 = (f32[128,63,128]{2,1,0:T(8,128)}, f32[128,63,128]{2,1,0:T(8,128)}) fusion(f32[128,64,128]{2,1,0:T(8,128)} %copy-done.2), kind=kLoop, calls=%fused_computation.260 | loop fusion | bytes 16515072 | tf_op jit(solution)/shard_map/jit(_roll_static)/slice | solution.py:111
  103.5 21.1 %fusion.83 = f32[128,64,128]{2,1,0:T(8,128)} fusion(f32[128,64,128]{2,1,0:T(8,128)} %copy-done.2, f32[1,64,128]{2,1,0:T(8,128)S(1)} %collective-permute-done.5, f32[1,64,128]{2,1,0:T(8,128)S(1)} %collective-permute-done.4, f32[128,64,128]{2,1,0:T(8,128)} %get-tuple-element.9, f32[128,1,128]{2,1,0:T(1,128)S(1)} %get-tuple-element.75, ...), kind=kLoop, calls=%fused_computation.96 | loop fusion | flops 31457280 | bytes 46268416 | tf_op jit(solution)/shard_map/add | solution.py:118
  124.6 8.2 %fusion.198 = (f32[128,64,1]{2,1,0:T(8,128)}, f32[128,64,1]{2,1,0:T(8,128)}) fusion(f32[128,64,128]{2,1,0:T(8,128)} %fusion.83), kind=kLoop, calls=%fused_computation.252 | loop fusion | bytes 131072 | tf_op jit(solution)/shard_map/jit(_roll_static)/slice | solution.py:116
  132.8 4.6 fusion.199
  137.4 4.6 fusion.201
  146.0 21.2 %fusion.73 = f32[128,64,128]{2,1,0:T(8,128)} fusion(f32[128,64,128]{2,1,0:T(8,128)} %fusion.83, f32[1,64,128]{2,1,0:T(8,128)S(1)} %collective-permute-done.7, f32[1,64,128]{2,1,0:T(8,128)S(1)} %collective-permute-done.6, f32[128,64,128]{2,1,0:T(8,128)} %get-tuple-element.9, f32[128,1,128]{2,1,0:T(1,128)S(1)} %get-tuple-element.65, ...), kind=kLoop, calls=%fused_computation.84 | loop fusion | flops 31457280 | bytes 46268416 | tf_op jit(solution)/shard_map/add | solution.py:118
  167.2 8.2 %fusion.193 = (f32[128,64,1]{2,1,0:T(8,128)}, f32[128,64,1]{2,1,0:T(8,128)}) fusion(f32[128,64,128]{2,1,0:T(8,128)} %fusion.73), kind=kLoop, calls=%fused_computation.247 | loop fusion | bytes 131072 | tf_op jit(solution)/shard_map/jit(_roll_static)/slice | solution.py:116
  175.5 4.6 fusion.194
  180.1 4.6 fusion.196
  188.3 21.1 %fusion.63 = f32[128,64,128]{2,1,0:T(8,128)} fusion(f32[128,64,128]{2,1,0:T(8,128)} %fusion.73, f32[1,64,128]{2,1,0:T(8,128)S(1)} %collective-permute-done.9, f32[1,64,128]{2,1,0:T(8,128)S(1)} %collective-permute-done.8, f32[128,64,128]{2,1,0:T(8,128)} %get-tuple-element.9, f32[128,1,128]{2,1,0:T(1,128)S(1)} %get-tuple-element.55, ...), kind=kLoop, calls=%fused_computation.72 | loop fusion | flops 31457280 | bytes 46268416 | tf_op jit(solution)/shard_map/add | solution.py:118
  209.4 8.2 %fusion.188 = (f32[128,64,1]{2,1,0:T(8,128)}, f32[128,64,1]{2,1,0:T(8,128)}) fusion(f32[128,64,128]{2,1,0:T(8,128)} %fusion.63), kind=kLoop, calls=%fused_computation.242 | loop fusion | bytes 131072 | tf_op jit(solution)/shard_map/jit(_roll_static)/slice | solution.py:116
  222.2 4.6 fusion.191
  230.5 21.2 %fusion.53 = f32[128,64,128]{2,1,0:T(8,128)} fusion(f32[128,64,128]{2,1,0:T(8,128)} %fusion.63, f32[1,64,128]{2,1,0:T(8,128)S(1)} %collective-permute-done.11, f32[1,64,128]{2,1,0:T(8,128)S(1)} %collective-permute-done.10, f32[128,64,128]{2,1,0:T(8,128)} %get-tuple-element.9, f32[128,1,128]{2,1,0:T(1,128)S(1)} %get-tuple-element.45, ...), kind=kLoop, calls=%fused_computation.60 | loop fusion | flops 31457280 | bytes 46268416 | tf_op jit(solution)/shard_map/add | solution.py:118
  251.7 8.2 %fusion.183 = (f32[128,64,1]{2,1,0:T(8,128)}, f32[128,64,1]{2,1,0:T(8,128)}) fusion(f32[128,64,128]{2,1,0:T(8,128)} %fusion.53), kind=kLoop, calls=%fused_computation.237 | loop fusion | bytes 131072 | tf_op jit(solution)/shard_map/jit(_roll_static)/slice | solution.py:116
  272.8 21.2 %fusion.43 = f32[128,64,128]{2,1,0:T(8,128)} fusion(f32[128,64,128]{2,1,0:T(8,128)} %fusion.53, f32[1,64,128]{2,1,0:T(8,128)S(1)} %collective-permute-done.13, f32[1,64,128]{2,1,0:T(8,128)S(1)} %collective-permute-done.12, f32[128,64,128]{2,1,0:T(8,128)} %get-tuple-element.9, f32[128,1,128]{2,1,0:T(1,128)S(1)} %get-tuple-element.35, ...), kind=kLoop, calls=%fused_computation.48 | loop fusion | flops 31457280 | bytes 46268416 | tf_op jit(solution)/shard_map/add | solution.py:118
  294.0 8.2 %fusion.178 = (f32[128,64,1]{2,1,0:T(8,128)}, f32[128,64,1]{2,1,0:T(8,128)}) fusion(f32[128,64,128]{2,1,0:T(8,128)} %fusion.43), kind=kLoop, calls=%fused_computation.232 | loop fusion | bytes 131072 | tf_op jit(solution)/shard_map/jit(_roll_static)/slice | solution.py:116
  315.1 21.1 %fusion.33 = f32[128,64,128]{2,1,0:T(8,128)} fusion(f32[128,64,128]{2,1,0:T(8,128)} %fusion.43, f32[1,64,128]{2,1,0:T(8,128)S(1)} %collective-permute-done.15, f32[1,64,128]{2,1,0:T(8,128)S(1)} %collective-permute-done.14, f32[128,64,128]{2,1,0:T(8,128)} %get-tuple-element.9, f32[128,1,128]{2,1,0:T(1,128)S(1)} %get-tuple-element.25, ...), kind=kLoop, calls=%fused_computation.36 | loop fusion | flops 31457280 | bytes 46268416 | tf_op jit(solution)/shard_map/add | solution.py:118
  336.2 8.2 %fusion.173 = (f32[128,64,1]{2,1,0:T(8,128)}, f32[128,64,1]{2,1,0:T(8,128)}) fusion(f32[128,64,128]{2,1,0:T(8,128)} %fusion.33), kind=kLoop, calls=%fused_computation.227 | loop fusion | bytes 131072 | tf_op jit(solution)/shard_map/jit(_roll_static)/slice | solution.py:116
  344.4 4.8 fusion.174
  357.6 22.4 %fusion.19 = f32[128,128,64]{1,2,0:T(8,128)} fusion(f32[64,64,1]{1,0,2:T(8,128)S(1)} %copy-done.16, f32[128,64,128]{2,1,0:T(8,128)} %fusion.33, f32[1,64,128]{2,1,0:T(8,128)S(1)} %collective-permute-done.17, f32[1,64,128]{2,1,0:T(8,128)S(1)} %collective-permute-done.16, f32[128,64,128]{2,1,0:T(8,128)} %get-tuple-element.9, ...), kind=kOutput, calls=%fused_computation.22 | convolution fusion | flops 836763648 | bytes 46284800 | tf_op jit(solution)/shard_map/vy,xyz->xvz/dot_general | solution.py:75
  380.0 8.2 %fusion.150 = f32[128,64,128]{2,0,1:T(8,128)S(1)} fusion(f32[128,128,1]{1,0,2:T(8,128)S(1)} %copy-done.14, f32[128,128,64]{1,2,0:T(8,128)} %fusion.19), kind=kOutput, calls=%fused_computation.200 | convolution fusion | flops 1610612736 | bytes 8454144 | tf_op jit(solution)/shard_map/xyz,wz->xyw/dot_general | solution.py:79
  388.3 5.6 all_gather.6
  402.0 156.9 %all-reduce.2.cloned.1.call-done = f32[128,64,128]{2,0,1:T(8,128)} async-done(((f32[128,64,128]{2,0,1:T(8,128)}), f32[128,64,128]{2,0,1:T(8,128)}) %all-reduce.2.cloned.1.call-update) | async-done | bytes 4194320 | tf_op jit(solution)/shard_map/psum | solution.py:136
  563.3 5.6 all_gather.7
  573.5 6.6 %fusion.153 = f32[128,128,64]{1,2,0:T(8,128)S(1)} fusion(f32[64,64,1]{1,0,2:T(8,128)S(1)} %copy-done.15, f32[128,64,128]{2,0,1:T(8,128)S(1)} %fusion.4), kind=kOutput, calls=%fused_computation.203 | convolution fusion | flops 805306368 | bytes 8404992 | tf_op jit(solution)/shard_map/vy,xyz->xvz/dot_general | solution.py:75
  580.1 7.1 %fusion.156 = f32[1,128,64,128]{3,1,2,0:T(8,128)S(1)} fusion(f32[128,128,1]{1,0,2:T(8,128)S(1)} %copy-done.13, f32[128,128,64]{1,2,0:T(8,128)S(1)} %fusion.153), kind=kOutput, calls=%fused_computation.206 | convolution fusion | flops 1610612736 | bytes 8454144 | tf_op jit(solution)/shard_map/xyz,wz->xyw/dot_general | solution.py:79
  (129 shorter events, 87.3 us)
Async XLA Ops:
  6.5 552.4 %all-reduce.2.cloned.1.call-start = ((), (), s32[]{:S(2)}) async-start(), calls=%async_computation | async-start | bytes 8388608 | tf_op jit(solution)/shard_map/psum | solution.py:136
  7.3 36.7 %collective-permute-start = (f32[1,64,128]{2,1,0:T(8,128)S(1)}, f32[1,64,128]{2,1,0:T(8,128)S(1)}, u32[]{:S(2)}, u32[]{:S(2)}) collective-permute-start(f32[1,64,128]{2,1,0:T(8,128)S(1)} %get-tuple-element.89), channel_id=1, source_target_pairs={{1,0},{2,1},{3,2},{0,3},{5,4},{6,5},{7,6},{4,7},{9,8},{10,9},{11,1... | collective-permute-start | bytes 98312 | tf_op jit(solution)/shard_map/ppermute | solution.py:18
  9.7 34.3 %collective-permute-start.2 = (f32[1,64,128]{2,1,0:T(8,128)S(1)}, f32[1,64,128]{2,1,0:T(8,128)S(1)}, u32[]{:S(2)}, u32[]{:S(2)}) collective-permute-start(f32[1,64,128]{2,1,0:T(8,128)S(1)} %get-tuple-element.88), channel_id=1, source_target_pairs={{0,1},{1,2},{2,3},{3,0},{4,5},{5,6},{6,7},{7,4},{8,9},{9,10},{10,1... | collective-permute-start | bytes 98312 | tf_op jit(solution)/shard_map/ppermute | solution.py:17
  10.5 33.6 %collective-permute-start.1 = (f32[1,64,128]{2,1,0:T(8,128)S(1)}, f32[1,64,128]{2,1,0:T(8,128)S(1)}, u32[]{:S(2)}, u32[]{:S(2)}) collective-permute-start(f32[1,64,128]{2,1,0:T(8,128)S(1)} %get-tuple-element.98), channel_id=1, source_target_pairs={{1,0},{2,1},{3,2},{0,3},{5,4},{6,5},{7,6},{4,7},{9,8},{10,9},{11,1... | collective-permute-start | bytes 98312 | tf_op jit(solution)/shard_map/ppermute | solution.py:18
  12.2 31.8 %collective-permute-start.3 = (f32[1,64,128]{2,1,0:T(8,128)S(1)}, f32[1,64,128]{2,1,0:T(8,128)S(1)}, u32[]{:S(2)}, u32[]{:S(2)}) collective-permute-start(f32[1,64,128]{2,1,0:T(8,128)S(1)} %get-tuple-element.99), channel_id=1, source_target_pairs={{0,1},{1,2},{2,3},{3,0},{4,5},{5,6},{6,7},{7,4},{8,9},{9,10},{10,1... | collective-permute-start | bytes 98312 | tf_op jit(solution)/shard_map/ppermute | solution.py:17
  12.2 12.9 %copy-start = (f32[1,128,64,128]{3,2,1,0:T(8,128)S(1)}, f32[1,128,64,128]{3,2,1,0:T(8,128)}, u32[]{:S(2)}) copy-start(f32[1,128,64,128]{3,2,1,0:T(8,128)} %param.16) | copy-start | bytes 12582916
  12.2 12.9 %copy-start.9 = (f32[1,128,64,128]{3,2,1,0:T(8,128)S(1)}, f32[1,128,64,128]{3,2,1,0:T(8,128)}, u32[]{:S(2)}) copy-start(f32[1,128,64,128]{3,2,1,0:T(8,128)} %param.15) | copy-start | bytes 12582916
  32.2 8.6 %copy-start.23 = (s32[64]{0:T(128)S(1)}, s32[64]{0:T(128)}, u32[]{:S(2)}) copy-start(s32[64]{0:T(128)} %constant.51.clone) | copy-start | bytes 772
  32.2 10.0 %copy-start.22 = (s32[128]{0:T(128)S(1)}, s32[128]{0:T(128)}, u32[]{:S(2)}) copy-start(s32[128]{0:T(128)} %constant.54.clone) | copy-start | bytes 1540
  88.4 15.0 %copy-start.1 = (f32[1,128,64,128]{3,2,1,0:T(8,128)S(1)}, f32[1,128,64,128]{3,2,1,0:T(8,128)}, u32[]{:S(2)}) copy-start(f32[1,128,64,128]{3,2,1,0:T(8,128)} %param.16) | copy-start | bytes 12582916
  98.1 3.3 collective-permute-start.4
  99.8 3.6 collective-permute-start.5
  124.6 8.2 %copy-start.4 = (f32[128,64,128]{2,1,0:T(8,128)S(1)}, f32[128,64,128]{2,1,0:T(8,128)}, u32[]{:S(2)}) copy-start(f32[128,64,128]{2,1,0:T(8,128)} %fusion.83) | copy-start | bytes 12582916
  142.1 1.7 collective-permute-start.6
  142.1 3.9 collective-permute-start.7
  167.2 8.2 %copy-start.5 = (f32[128,64,128]{2,1,0:T(8,128)S(1)}, f32[128,64,128]{2,1,0:T(8,128)}, u32[]{:S(2)}) copy-start(f32[128,64,128]{2,1,0:T(8,128)} %fusion.73) | copy-start | bytes 12582916
  184.7 1.6 collective-permute-start.8
  184.7 3.6 collective-permute-start.9
  209.4 8.2 %copy-start.6 = (f32[128,64,128]{2,1,0:T(8,128)S(1)}, f32[128,64,128]{2,1,0:T(8,128)}, u32[]{:S(2)}) copy-start(f32[128,64,128]{2,1,0:T(8,128)} %fusion.63) | copy-start | bytes 12582916
  226.8 1.7 collective-permute-start.10
  226.9 3.5 collective-permute-start.11
  269.1 1.8 collective-permute-start.12
  269.2 3.6 collective-permute-start.13
  294.0 8.2 %copy-start.8 = (f32[128,64,128]{2,1,0:T(8,128)S(1)}, f32[128,64,128]{2,1,0:T(8,128)}, u32[]{:S(2)}) copy-start(f32[128,64,128]{2,1,0:T(8,128)} %fusion.43) | copy-start | bytes 12582916
  311.4 1.7 collective-permute-start.14
  311.5 3.6 collective-permute-start.15
  349.1 8.5 %copy-start.16 = (f32[64,64,1]{1,0,2:T(8,128)S(1)}, f32[64,64,1]{1,0,2:T(8,128)}, u32[]{:S(2)}) copy-start(f32[64,64,1]{1,0,2:T(8,128)} %constant.64) | copy-start | bytes 49156
  353.7 1.6 collective-permute-start.16
  353.7 3.9 collective-permute-start.17
  357.6 22.4 %copy-start.14 = (f32[128,128,1]{1,0,2:T(8,128)S(1)}, f32[128,128,1]{1,0,2:T(8,128)}, u32[]{:S(2)}) copy-start(f32[128,128,1]{1,0,2:T(8,128)} %constant.65) | copy-start | bytes 196612
  380.0 14.0 %copy-start.19 = (f32[4,4,1]{1,0,2:T(4,128)S(1)}, f32[4,4,1]{1,0,2:T(4,128)}, u32[]{:S(2)}) copy-start(f32[4,4,1]{1,0,2:T(4,128)} %constant.66) | copy-start | bytes 196
  380.0 14.5 %copy-start.12 = (f32[128,129,1]{0,1,2:T(8,128)S(1)}, f32[128,129,1]{0,1,2:T(8,128)}, u32[]{:S(2)}) copy-start(f32[128,129,1]{0,1,2:T(8,128)} %constant.67) | copy-start | bytes 198148
  (11 other events, 69.0 us)
Sparse Core Ops, SparseCore 0:
  402.1 156.7 all-reduce.1
where the time goes:
time: 608 us; the launch traced here: 599 us
  waiting for transfers between devices  176 us (29%)
  other arithmetic  172 us (28%)
  local copies, waits for them, and re-layouts  161 us (26%)
  matrix products  53.5 us (9%)
  between operations  14.9 us (2%)
  blocking collectives  11.2 us (2%)
  starting transfers between devices  11 us (2%)
    add x7, other arithmetic, local(): field = field + flux  162 us
    psum x1, waiting for transfers between devices, local(): total = lax.psum(weight * mask * surplus, 'grid')  157 us
    slice x14, local copies, waits for them, and re-layouts, local(): jnp.roll(field, 1, 2) - field  86.8 us
    slice x14, local copies, waits for them, and re-layouts, local(): jnp.roll(field, 1, 1) - field  38.2 us
    dot_general x2, matrix products, along_second(): jnp.einsum('vy,xyz->xvz', matrix, field, precision=lax.Precision.HIGHEST)  29 us
    dot_general x2, matrix products, along_third(): jnp.einsum('xyz,wz->xyw', field, matrix, precision=lax.Precision.HIGHEST)  15.4 us
    ppermute x9, waiting for transfers between devices, extended_2(): before = lax.ppermute(last, axis, up)  14.5 us
    slice x2, local copies, waits for them, and re-layouts, local(): face_zp = 0.5 * (coeff + jnp.roll(coeff, -1, 2))  14.1 us
  transfers between devices with their start and end apart: 19, of which 14 were waited for; matrix products, arithmetic and copies ran while one was open for 6% of the time, Pallas kernels for 0%

commit v1 on v0

v1 whole, which is shorter than its diff:
```python
import functools

import jax
import jax.numpy as jnp
import numpy as np
from jax import lax
from jax.experimental import pallas as pl
from jax.experimental.pallas import tpu as pltpu
from jax.sharding import PartitionSpec as P

ITERS = 8
BASE = 3
EXTRA = 3
TOP = BASE + EXTRA
LANES = 128
VMEM_LIMIT = 56 * 1024 * 1024


def trailing_zeros(index):
    return (index & -index).bit_length() - 1


def level_of(index, count):
    return 0 if index == 0 else count.bit_length() - 1 - trailing_zeros(index)


def excess_of(index, count):
    return max(level_of(index, count) - BASE, 0)


def kept_indices(count):
    kept = [i for i in range(count) if level_of(i, count) <= TOP]
    return sorted(kept, key=lambda i: (excess_of(i, count), i))


def matrices(count):
    depth = count.bit_length() - 1
    hier = np.eye(count)
    dehier = np.eye(count)
    for index in range(1, count):
        spacing = 1 << trailing_zeros(index)
        hier[index, (index - spacing) % count] -= 0.5
        hier[index, (index + spacing) % count] -= 0.5
    for trailing in range(depth - 1, -1, -1):
        spacing = 1 << trailing
        for index in range(spacing, count, 2 * spacing):
            dehier[index] += 0.5 * (dehier[(index - spacing) % count] + dehier[(index + spacing) % count])
    return hier, dehier


def axis_tables(width_y, width_z):
    hier_y, dehier_y = matrices(width_y)
    hier_z, dehier_z = matrices(width_z)
    kept_y, kept_z = kept_indices(width_y), kept_indices(width_z)
    groups = width_y // 8
    order = [s * groups + j for j in range(groups) for s in range(8)]
    hy = hier_y[kept_y][:, order]
    dy = dehier_y[:, kept_y]
    hz = np.zeros((width_z, LANES))
    hz[:, : len(kept_z)] = hier_z[kept_z].T
    dz = np.zeros((LANES, width_z))
    dz[: len(kept_z)] = dehier_z[:, kept_z].T
    level_y = np.array([level_of(i, width_y) for i in kept_y])
    level_z = np.full(LANES, 99)
    level_z[: len(kept_z)] = [level_of(i, width_z) for i in kept_z]
    shape = (len(kept_y), LANES)
    ly = np.broadcast_to(level_y[:, None], shape).astype(np.int32)
    lz = np.broadcast_to(level_z[None, :], shape).astype(np.int32)
    as_bf16 = lambda m: jnp.asarray(m, jnp.bfloat16)
    return as_bf16(hy), as_bf16(hz), as_bf16(dy), as_bf16(dz), jnp.asarray(ly), jnp.asarray(lz)


class Plan:
    def __init__(self, members, slab, width_y, width_z):
        width_x = members * slab
        self.members = members
        self.stride = max(1, width_x >> TOP)
        self.rows = slab // self.stride
        kept_y = kept_indices(width_y)
        kept_z = kept_indices(width_z)
        self.blocks = len(kept_y) // 8
        block_excess = [max(excess_of(i, width_y) for i in kept_y[8 * q : 8 * q + 8]) for q in range(self.blocks)]
        width_of = [sum(excess_of(i, width_z) <= e for i in kept_z) for e in range(EXTRA + 1)]
        indices = [p * slab for p in range(members)] + [k * self.stride for k in range(1, self.rows)]
        self.levels = [level_of(i, width_x) for i in indices]
        pieces = []
        for row, index in enumerate(indices):
            for q in range(self.blocks):
                left = EXTRA - excess_of(index, width_x) - block_excess[q]
                if left >= 0:
                    pieces.append((width_of[left], row, q))
        pieces.sort(key=lambda piece: (-piece[0], piece[1], piece[2]))
        self.pieces, at = [], 0
        for width, row, q in pieces:
            if at % LANES + width > LANES:
                at += LANES - at % LANES
            self.pieces.append((row, q, at // LANES, at % LANES))
            at += width
        self.tiles = -(-at // LANES)


def split_dot(left, right, exact_left):
    value = right if exact_left else left
    high = value.astype(jnp.bfloat16)
    low = (value - high.astype(jnp.float32)).astype(jnp.bfloat16)
    dot = functools.partial(jnp.dot, preferred_element_type=jnp.float32)
    if exact_left:
        return dot(left, high) + dot(left, low)
    return dot(high, right) + dot(low, right)


def next_lane(v):
    return pltpu.roll(v, LANES - 1, 1)


def last_lane(v):
    return pltpu.roll(v, 1, 1)


def row_update(f, above, flux_below, fx, fy, fz, groups):
    gx = [fx[j] * (above[j] - f[j]) for j in range(groups)]
    follow = f[1:] + [pltpu.roll(f[0], 7, 0)]
    gy = [fy[j] * (follow[j] - f[j]) for j in range(groups)]
    before = [pltpu.roll(gy[-1], 1, 0)] + gy[:-1]
    new = []
    for j in range(groups):
        gz = fz[j] * (next_lane(f[j]) - f[j])
        plus = (f[j] + gx[j]) + (gy[j] + gz)
        minus = (flux_below[j] + before[j]) + last_lane(gz)
        new.append(plus - minus)
    return new, gx


def diffuse_kernel(plan, slab, groups, chunk, dens, kap, dprev, kprev, dnext, knext, hy, hz, out, raw_d, raw_k, f, fx, fy, fz, sems):
    halo = ITERS
    chunks = slab // chunk
    copies = []
    for c in range(chunks):
        part = pl.ds(c * chunk, chunk)
        pair = (
            pltpu.make_async_copy(kap.at[0, part], raw_k.at[part], sems.at[0, c]),
            pltpu.make_async_copy(dens.at[0, part], raw_d.at[part], sems.at[1, c]),
        )
        for copy in pair:
            copy.start()
        copies.append(pair)

    def natural(ref, row):
        return [ref[row, pl.ds(j, 8, stride=groups), :] for j in range(groups)]

    def stored(ref, row):
        return [ref[row, j] for j in range(groups)]

    def put(ref, row, values):
        for j in range(groups):
            ref[row, j] = values[j]

    def first(r, k_above, d_above, carry):
        k, d, flux = carry
        x_face = [0.5 * (k[j] + k_above[j]) for j in range(groups)]
        k_next = k[1:] + [pltpu.roll(k[0], 7, 0)]
        y_face = [0.5 * (k[j] + k_next[j]) for j in range(groups)]
        z_face = [0.5 * (k[j] + next_lane(k[j])) for j in range(groups)]
        put(fx, r - 1, x_face)
        put(fy, r - 1, y_face)
        put(fz, r - 1, z_face)
        new, flux = row_update(d, d_above, flux, x_face, y_face, z_face, groups)
        put(f, r - 1, new)
        return k_above, d_above, flux

    zero = [jnp.zeros((8, LANES), jnp.float32)] * groups
    carry = (natural(kprev, 0), natural(dprev, 0), zero)
    carry = lax.fori_loop(1, halo, lambda r, c: first(r, natural(kprev, r), natural(dprev, r), c), carry)
    for c in range(chunks):
        for copy in copies[c]:
            copy.wait()
        carry = lax.fori_loop(
            halo + c * chunk,
            halo + (c + 1) * chunk,
            lambda r, v: first(r, natural(raw_k, r - halo), natural(raw_d, r - halo), v),
            carry,
        )
    first(slab + halo, natural(knext, 0), natural(dnext, 0), carry)

    stride = plan.stride
    left = ITERS - 2
    while 2 * left + 1 >= stride:
        low, high = halo - left, halo + slab - stride + left
        low -= (high - low + 1) % 2

        def pair_step(i, carry, low=low):
            row, flux = carry
            for u in range(2):
                r = low + 2 * i + u
                above = stored(f, r + 1)
                new, flux = row_update(row, above, flux, stored(fx, r), stored(fy, r), stored(fz, r), groups)
                put(f, r, new)
                row = above
            return row, flux

        row = stored(f, low)
        below = stored(f, low - 1)
        face = stored(fx, low - 1)
        flux = [face[j] * (row[j] - below[j]) for j in range(groups)]
        lax.fori_loop(0, (high - low + 1) // 2, pair_step, (row, flux))
        left -= 1

    def cone(center, wanted, left):
        def near(j, reach):
            return any(min((j - w) % groups, (w - j) % groups) <= reach for w in wanted)

        for reach in range(left, -1, -1):
            flux = {}
            for offset in range(-reach, reach + 1):
                need = [j for j in range(groups) if near(j, reach - abs(offset))]
                r = center + offset
                cells = {}

                def cell(j):
                    if j not in cells:
                        cells[j] = f[r, j]
                    return cells[j]

                below, flux, fluxes_y, results = flux, {}, {}, {}

                def flux_y(j):
                    if j not in fluxes_y:
                        follow = cell(j + 1) if j + 1 < groups else pltpu.roll(cell(0), 7, 0)
                        fluxes_y[j] = fy[r, j] * (follow - cell(j))
                    return fluxes_y[j]

                for j in need:
                    here = cell(j)
                    flux[j] = fx[r, j] * (f[r + 1, j] - here)
                    lower = below[j] if j in below else fx[r - 1, j] * (here - f[r - 1, j])
                    before = flux_y(j - 1) if j else pltpu.roll(flux_y(groups - 1), 1, 0)
                    gz = fz[r, j] * (next_lane(here) - here)
                    results[j] = ((here + flux[j]) + (flux_y(j) + gz)) - ((lower + before) + last_lane(gz))
                for j in need:
                    f[r, j] = results[j]

    period = min(4, plan.rows)

    def cones(i, _):
        for k in range(period):
            spare = EXTRA - (0 if k == 0 else max(0, EXTRA - trailing_zeros(k)))
            if k == 0 and period < 4:
                spare = EXTRA
            step = max(1, groups >> spare)
            cone(halo + (i * period + k) * stride, list(range(0, groups, step)), left)
        return 0

    lax.fori_loop(0, plan.rows // period, cones, 0)

    for k in range(plan.rows):
        plane = f[halo + k * stride].reshape(groups * 8, LANES)
        out[k] = split_dot(split_dot(hy[...], plane, True), hz[...], False)


def grid_mask(levels, ly, lz):
    return (ly[...] <= levels[0, 1]) & (lz[...] <= levels[0, 2])


def pack_kernel(plan, pos_ref, levels, coefs, ly, lz, planes, coarse, out):
    mask = grid_mask(levels, ly, lz)
    weight = coefs[0].astype(jnp.float32)
    members, rows = plan.members, plan.rows
    surplus = []
    for p in range(members):
        if p == 0:
            value = coarse[0]
        else:
            h = 1 << trailing_zeros(p)
            value = coarse[p] - 0.5 * (coarse[p - h] + coarse[(p + h) % members])
        surplus.append(value)
    following = coarse[lax.rem(pos_ref[0] + 1, members)]
    for k in range(1, rows):
        h = 1 << trailing_zeros(k)
        above = planes[k + h] if k + h < rows else following
        surplus.append(planes[k] - 0.5 * (planes[k - h] + above))
    for row in range(len(surplus)):
        scale = jnp.where(plan.levels[row] <= levels[0, 0], weight, 0.0)
        surplus[row] = jnp.where(mask, scale * surplus[row], 0.0)
    tiles = [None] * plan.tiles
    for row, q, tile, lane in plan.pieces:
        piece = surplus[row][8 * q : 8 * q + 8]
        if lane:
            piece = pltpu.roll(piece, lane, 1)
        tiles[tile] = piece if tiles[tile] is None else tiles[tile] + piece
    for tile in range(plan.tiles):
        out[tile] = tiles[tile]


def expand_kernel(plan, slab, pos_ref, levels, ly, lz, dy, dz, packed, out, coarse, nodes, buf, sems):
    mask = grid_mask(levels, ly, lz)
    members, rows, stride = plan.members, plan.rows, plan.stride
    where = {(row, q): (tile, lane) for row, q, tile, lane in plan.pieces}

    def total(row):
        parts = []
        for q in range(plan.blocks):
            if (row, q) in where:
                tile, lane = where[row, q]
                piece = packed[tile]
                if lane:
                    piece = pltpu.roll(piece, LANES - lane, 1)
                keep = mask[8 * q : 8 * q + 8] & (plan.levels[row] <= levels[0, 0])
                parts.append(jnp.where(keep, piece, 0.0))
            else:
                parts.append(jnp.zeros((8, LANES), jnp.float32))
        return jnp.concatenate(parts, axis=0)

    values = [total(p) for p in range(members)]
    h = members // 2
    while h:
        for p in range(h, members, 2 * h):
            values[p] = values[p] + 0.5 * (values[p - h] + values[(p + h) % members])
        h //= 2
    for p in range(members):
        coarse[p] = values[p]
    pos = pos_ref[0]
    fine = [coarse[pos]] + [total(members + k - 1) for k in range(1, rows)] + [coarse[lax.rem(pos + 1, members)]]
    h = rows // 2
    while h:
        for k in range(h, rows, 2 * h):
            fine[k] = fine[k] + 0.5 * (fine[k - h] + fine[k + h])
        h //= 2
    for k in range(rows + 1):
        nodes[k] = split_dot(dy[...], split_dot(fine[k], dz[...], False), True)

    def chunk(k):
        part = pl.ds(k * stride, stride)
        return pltpu.make_async_copy(buf.at[part], out.at[0, part], sems.at[k])

    def fill(k, _):
        here = nodes[k]
        step = (nodes[k + 1] - here) * (1.0 / stride)
        for j in range(stride):
            buf[k * stride + j] = here + float(j) * step if j else here
        chunk(k).start()
        return 0

    lax.fori_loop(0, rows, fill, 0)

    def drain(k, _):
        chunk(k).wait()
        return 0

    lax.fori_loop(0, rows, drain, 0)


def local(plan, density, kappa, levels, coefs):
    _, slab, width_y, width_z = density.shape
    groups = width_y // 8
    members = lax.axis_size("space")
    position = lax.axis_index("space")
    hy, hz, dy, dz, ly, lz = axis_tables(width_y, width_z)
    pos = jnp.reshape(position, (1,)).astype(jnp.int32)
    up = [(i, (i + 1) % members) for i in range(members)]
    down = [(j, i) for i, j in up]
    dprev = lax.ppermute(density[0, slab - ITERS :], "space", up)
    kprev = lax.ppermute(kappa[0, slab - ITERS :], "space", up)
    dnext = lax.ppermute(density[0, :1], "space", down)
    knext = lax.ppermute(kappa[0, :1], "space", down)

    vmem = pl.BlockSpec(memory_space=pltpu.VMEM)
    smem = pl.BlockSpec(memory_space=pltpu.SMEM)
    anywhere = pl.BlockSpec(memory_space=pl.ANY)
    params = pltpu.CompilerParams(vmem_limit_bytes=VMEM_LIMIT)
    kept = ly.shape[0]
    chunk = min(32, slab)
    extended = pltpu.VMEM((slab + ITERS, groups, 8, LANES), jnp.float32)
    raw = pltpu.VMEM((slab, width_y, width_z), jnp.float32)
    planes = pl.pallas_call(
        functools.partial(diffuse_kernel, plan, slab, groups, chunk),
        out_shape=jax.ShapeDtypeStruct((plan.rows, kept, LANES), jnp.float32),
        in_specs=[anywhere, anywhere] + [vmem] * 6,
        out_specs=vmem,
        scratch_shapes=[raw, raw, extended, extended, extended, extended, pltpu.SemaphoreType.DMA((2, slab // chunk))],
        compiler_params=params,
        name="diffuse",
    )(density, kappa, dprev, kprev, dnext, knext, hy, hz)

    coarse = lax.all_gather(planes[0], "space", axis=0)
    packed = pl.pallas_call(
        functools.partial(pack_kernel, plan),
        out_shape=jax.ShapeDtypeStruct((plan.tiles, 8, LANES), jnp.float32),
        in_specs=[smem, smem, smem] + [vmem] * 4,
        out_specs=vmem,
        compiler_params=params,
        name="pack",
    )(pos, levels, coefs, ly, lz, planes, coarse)

    packed = lax.psum(packed, "grid")

    return pl.pallas_call(
        functools.partial(expand_kernel, plan, slab),
        out_shape=jax.ShapeDtypeStruct(density.shape, jnp.float32),
        in_specs=[smem, smem] + [vmem] * 5,
        out_specs=anywhere,
        scratch_shapes=[
            pltpu.VMEM((plan.members, kept, LANES), jnp.float32),
            pltpu.VMEM((plan.rows + 1, width_y, width_z), jnp.float32),
            raw,
            pltpu.SemaphoreType.DMA((plan.rows,)),
        ],
        compiler_params=params,
        name="expand",
    )(pos, levels, ly, lz, dy, dz, packed)


def solution(mesh):
    def whole(density, kappa, levels, coefs):
        members = mesh.shape["space"]
        plan = Plan(members, density.shape[1] // members, density.shape[2], density.shape[3])
        in_specs = (
            P("grid", "space", None, None),
            P("grid", "space", None, None),
            P("grid", None),
            P("grid"),
        )
        out_specs = P("grid", "space", None, None)
        body = functools.partial(local, plan)
        return jax.shard_map(body, mesh=mesh, in_specs=in_specs, out_specs=out_specs, check_vma=False)(density, kappa, levels, coefs)

    return whole
```

time: 608 us -> 129 us (0.21); the launches traced: 599 us -> 129 us
  waiting for transfers between devices: 176 us -> 3.56 us
  other arithmetic: 172 us -> 0 us
  local copies, waits for them, and re-layouts: 161 us -> 4.92 us
  Pallas kernels: 0 us -> 70.8 us
  matrix products: 53.5 us -> 0 us
  blocking collectives: 11.2 us -> 45.7 us
  between operations: 14.9 us -> 0.69 us
  starting transfers between devices: 11 us -> 3.19 us
    add x7 -> x0, other arithmetic: 162 us -> none  [local(): field = field + flux]
    psum x1 -> x0, waiting for transfers between devices: 157 us -> none  [local(): total = lax.psum(weight * mask * surplus, 'grid')]
    slice x45 -> x1, local copies, waits for them, and re-layouts: 156 us -> 0.76 us  [local(): coarse = lax.all_gather(planes[0], 'space', axis=0)]
    pallas_call x0 -> x3, Pallas kernels: none -> 70.8 us  [the longest x1 62.8 us: local(): pl.pallas_call(functools.partial(diffuse_kernel, plan, slab, groups, chun...]
    dot_general x8 -> x0, matrix products: 53.5 us -> none  [the longest x2 29 us: along_second(): jnp.einsum('vy,xyz->xvz', matrix, field, precision=lax.Precision.HIGHEST)]
    psum x0 -> x1, blocking collectives: none -> 39.4 us  [local(): packed = lax.psum(packed, 'grid')]
    ppermute x18 -> x4, waiting for transfers between devices: 19.1 us -> 3.56 us  [the longest x1 2.36 us: local(): dprev = lax.ppermute(density[0, slab - ITERS:], 'space', up)]
    ppermute x18 -> x4, starting transfers between devices: 11 us -> 3.19 us  [the longest x1 2.65 us: local(): dprev = lax.ppermute(density[0, slab - ITERS:], 'space', up)]
  transfers between devices with their start and end apart: 19 -> 4, of which waited for: 14 -> 3; matrix products, arithmetic and copies ran while one was open for 6% -> 2% of each run, Pallas kernels for 0% -> 0%
where the time goes in v1:
time: 129 us
  Pallas kernels  70.8 us (55%)
  blocking collectives  45.7 us (35%)
  local copies, waits for them, and re-layouts  4.92 us (4%)
  waiting for transfers between devices  3.56 us (3%)
  starting transfers between devices  3.19 us (2%)
    pallas_call x1, Pallas kernels, local(): pl.pallas_call(functools.partial(diffuse_kernel, plan, slab, groups, chun...  62.8 us
    psum x1, blocking collectives, local(): packed = lax.psum(packed, 'grid')  39.4 us
    all_gather x1, blocking collectives, local(): coarse = lax.all_gather(planes[0], 'space', axis=0)  6.37 us
    pallas_call x1, Pallas kernels, local(): pl.pallas_call(functools.partial(expand_kernel, plan, slab), out_shape=ja...  6.14 us
    ppermute x1, starting transfers between devices, local(): dprev = lax.ppermute(density[0, slab - ITERS:], 'space', up)  2.65 us
  transfers between devices with their start and end apart: 4, of which 3 were waited for; matrix products, arithmetic and copies ran while one was open for 2% of the time, Pallas kernels for 0%

profile of v1, /device:TPU:0, one launch (start us, length us, event | category | flops | bytes accessed | tf_op | source)
XLA Modules:
  0.0 128.9 jit_solution(17402588498624525575)
XLA Ops:
  0.0 1.0 slice_bitcast_fusion
  1.0 0.5 collective-permute-start.1
  1.5 1.0 slice_bitcast_fusion.1
  2.4 2.7 %collective-permute-start = (f32[8,64,128]{2,1,0:T(8,128)S(1)}, f32[8,64,128]{2,1,0:T(8,128)S(1)}, u32[]{:S(2)}, u32[]{:S(2)}) collective-permute-start(f32[8,64,128]{2,1,0:T(8,128)S(1)} %slice_bitcast_fusion.1), channel_id=1, source_target_pairs={{0,1},{1,2},{2,3},{3,0},{4,5},{5,6},{6,7},{7,4},{8,9},{9,10},{10,1... | collective-permute-start | bytes 786440 | tf_op jit(solution)/shard_map/ppermute | solution.py:361
  5.1 0.8 slice_bitcast_fusion.2
  5.9 0.0 collective-permute-start.3
  5.9 0.8 slice_bitcast_fusion.3
  6.6 0.0 collective-permute-start.2
  7.3 0.4 collective-permute-done.3.knext
  7.7 0.0 copy-start.2
  7.7 0.8 collective-permute-done.2.dnext
  8.5 0.0 copy-start.3
  8.5 0.0 collective-permute-done.1.kprev
  8.5 0.0 copy-start
  8.5 2.4 %collective-permute-done.dprev = f32[8,64,128]{2,1,0:T(8,128)S(1)} collective-permute-done((f32[8,64,128]{2,1,0:T(8,128)S(1)}, f32[8,64,128]{2,1,0:T(8,128)S(1)}, u32[]{:S(2)}, u32[]{:S(2)}) %collective-permute-start) | collective-permute-done | bytes 262176 | tf_op jit(solution)/shard_map/ppermute | solution.py:361
  10.9 0.0 copy-done.2
  10.9 0.0 copy-done.3
  10.9 0.0 copy-done
  10.9 0.0 copy-start.1
  10.9 0.7 copy-done.1
  11.6 62.8 %diffuse.1.planes = f32[16,64,128]{2,1,0:T(8,128)} custom-call(f32[1,128,64,128]{3,2,1,0:T(8,128)} %dens.1, f32[1,128,64,128]{3,2,1,0:T(8,128)} %kap.1, f32[8,64,128]{2,1,0:T(8,128)} %copy-done.1, f32[8,64,128]{2,1,0:T(8,128)} %copy-done, f32[1,64,128]{2,1,0:T(8,128)} %copy-done.3, f32[1,64,128]{2,1,0:T(8,128)} %copy-done.2, ...), custom_call_target="tpu_custom_call" | custom-call | tf_op jit(solution)/shard_map/diffuse/pallas_call | solution.py:374
  74.4 0.8 slice.20
  75.1 6.4 %all_gather.3.coarse = f32[4,64,128]{2,1,0:T(8,128)} all-gather(f32[1,64,128]{2,1,0:T(8,128)S(1)} %slice.20), channel_id=1, replica_groups=mesh['grid'=8,'space'=4] {'space'}, dimensions={0}, use_global_device_ids=true | all-gather | bytes 163840 | tf_op jit(solution)/shard_map/all_gather | solution.py:384
  81.5 1.9 %pack.1 = f32[9,8,128]{2,1,0:T(8,128)} custom-call(s32[1]{0:T(128)} %bitcast.pos_ref, s32[1,3]{1,0:T(1,128)} %levels.3, s32[1]{0:T(128)S(6)} %copy.11.coefs, s32[64,128]{1,0:T(8,128)} %constant.20.clone.ly, s32[64,128]{1,0:T(8,128)} %constant.21.clone.lz, f32[16,64,128]{2,1,0:T(8,128)} %diffuse.1.planes, f32[4,64,128]{2,1,0:T(8,128)} %all_gather.3.coarse), custom_call_target="tpu_custom_call" | custom-call | tf_op jit(solution)/shard_map/pack/pallas_call | solution.py:385
  83.4 39.4 %psum.7.packed = f32[9,8,128]{2,1,0:T(8,128)} all-reduce(f32[9,8,128]{2,1,0:T(8,128)} %pack.1), channel_id=1, replica_groups=mesh['grid'=8,'space'=4] {'grid'}, use_global_device_ids=true, to_apply=%region_0.0 | all-reduce | flops 9216 | bytes 73728 | tf_op jit(solution)/shard_map/psum | solution.py:394
  122.7 6.1 %expand.1 = f32[1,128,64,128]{3,2,1,0:T(8,128)} custom-call(s32[1]{0:T(128)} %bitcast.pos_ref, s32[1,3]{1,0:T(1,128)} %levels.3, s32[64,128]{1,0:T(8,128)} %constant.20.clone.ly, s32[64,128]{1,0:T(8,128)} %constant.21.clone.lz, bf16[64,64]{1,0:T(8,128)(2,1)} %constant.18.clone.dy, bf16[128,128]{1,0:T(8,128)(2,1)} %constant.19.clone.dz, f32[9,8,128]{2,1,0:T(8,128)} %psum.7.packed), custom_call_target="tpu_custom_call" | custom-call | tf_op jit(solution)/shard_map/expand/pallas_call | solution.py:396
Async XLA Ops:
  1.0 7.5 %collective-permute-start.1 = (f32[8,64,128]{2,1,0:T(8,128)S(1)}, f32[8,64,128]{2,1,0:T(8,128)S(1)}, u32[]{:S(2)}, u32[]{:S(2)}) collective-permute-start(f32[8,64,128]{2,1,0:T(8,128)S(1)} %slice_bitcast_fusion), channel_id=1, source_target_pairs={{0,1},{1,2},{2,3},{3,0},{4,5},{5,6},{6,7},{7,4},{8,9},{9,10},{10,1... | collective-permute-start | bytes 786440 | tf_op jit(solution)/shard_map/ppermute | solution.py:362
  2.4 8.4 %collective-permute-start = (f32[8,64,128]{2,1,0:T(8,128)S(1)}, f32[8,64,128]{2,1,0:T(8,128)S(1)}, u32[]{:S(2)}, u32[]{:S(2)}) collective-permute-start(f32[8,64,128]{2,1,0:T(8,128)S(1)} %slice_bitcast_fusion.1), channel_id=1, source_target_pairs={{0,1},{1,2},{2,3},{3,0},{4,5},{5,6},{6,7},{7,4},{8,9},{9,10},{10,1... | collective-permute-start | bytes 786440 | tf_op jit(solution)/shard_map/ppermute | solution.py:361
  5.9 1.9 %collective-permute-start.3 = (f32[1,64,128]{2,1,0:T(8,128)S(1)}, f32[1,64,128]{2,1,0:T(8,128)S(1)}, u32[]{:S(2)}, u32[]{:S(2)}) collective-permute-start(f32[1,64,128]{2,1,0:T(8,128)S(1)} %slice_bitcast_fusion.2), channel_id=1, source_target_pairs={{1,0},{2,1},{3,2},{0,3},{5,4},{6,5},{7,6},{4,7},{9,8},{10,9},{11,1... | collective-permute-start | bytes 98312 | tf_op jit(solution)/shard_map/ppermute | solution.py:364
  6.6 1.9 %collective-permute-start.2 = (f32[1,64,128]{2,1,0:T(8,128)S(1)}, f32[1,64,128]{2,1,0:T(8,128)S(1)}, u32[]{:S(2)}, u32[]{:S(2)}) collective-permute-start(f32[1,64,128]{2,1,0:T(8,128)S(1)} %slice_bitcast_fusion.3), channel_id=1, source_target_pairs={{1,0},{2,1},{3,2},{0,3},{5,4},{6,5},{7,6},{4,7},{9,8},{10,9},{11,1... | collective-permute-start | bytes 98312 | tf_op jit(solution)/shard_map/ppermute | solution.py:363
  7.7 3.2 %copy-start.2 = (f32[1,64,128]{2,1,0:T(8,128)}, f32[1,64,128]{2,1,0:T(8,128)S(1)}, u32[]{:S(2)}) copy-start(f32[1,64,128]{2,1,0:T(8,128)S(1)} %collective-permute-done.3.knext) | copy-start | bytes 98308
  8.5 2.4 %copy-start.3 = (f32[1,64,128]{2,1,0:T(8,128)}, f32[1,64,128]{2,1,0:T(8,128)S(1)}, u32[]{:S(2)}) copy-start(f32[1,64,128]{2,1,0:T(8,128)S(1)} %collective-permute-done.2.dnext) | copy-start | bytes 98308
  8.5 2.4 %copy-start = (f32[8,64,128]{2,1,0:T(8,128)}, f32[8,64,128]{2,1,0:T(8,128)S(1)}, u32[]{:S(2)}) copy-start(f32[8,64,128]{2,1,0:T(8,128)S(1)} %collective-permute-done.1.kprev) | copy-start | bytes 786436
  10.9 0.7 copy-start.1

commit v2 on v1

--- a/solution.py
+++ b/solution.py
@@ -13,6 +13,7 @@
 EXTRA = 3
 TOP = BASE + EXTRA
 LANES = 128
+UNROLL = 8
 VMEM_LIMIT = 56 * 1024 * 1024
 
 
@@ -131,7 +132,7 @@
     return new, gx
 
 
-def diffuse_kernel(plan, slab, groups, chunk, dens, kap, dprev, kprev, dnext, knext, hy, hz, out, raw_d, raw_k, f, fx, fy, fz, sems):
+def diffuse_kernel(plan, slab, groups, chunk, dens, kap, dprev, kprev, dnext, knext, hy, hz, out, raw_d, raw_k, f_a, f_b, fx, fy, fz, sems):
     halo = ITERS
     chunks = slab // chunk
     copies = []
@@ -165,95 +166,104 @@
         put(fy, r - 1, y_face)
         put(fz, r - 1, z_face)
         new, flux = row_update(d, d_above, flux, x_face, y_face, z_face, groups)
-        put(f, r - 1, new)
+        put(f_a, r - 1, new)
         return k_above, d_above, flux
 
     zero = [jnp.zeros((8, LANES), jnp.float32)] * groups
     carry = (natural(kprev, 0), natural(dprev, 0), zero)
-    carry = lax.fori_loop(1, halo, lambda r, c: first(r, natural(kprev, r), natural(dprev, r), c), carry)
+    for r in range(1, halo):
+        carry = first(r, natural(kprev, r), natural(dprev, r), carry)
     for c in range(chunks):
         for copy in copies[c]:
             copy.wait()
-        carry = lax.fori_loop(
-            halo + c * chunk,
-            halo + (c + 1) * chunk,
-            lambda r, v: first(r, natural(raw_k, r - halo), natural(raw_d, r - halo), v),
-            carry,
-        )
+
+        def several(i, carry, c=c):
+            for u in range(UNROLL):
+                x = c * chunk + i * UNROLL + u
+                carry = first(x + halo, natural(raw_k, x), natural(raw_d, x), carry)
+            return carry
+
+        carry = lax.fori_loop(0, chunk // UNROLL, several, carry)
     first(slab + halo, natural(knext, 0), natural(dnext, 0), carry)
 
     stride = plan.stride
     left = ITERS - 2
+    old, new_f = f_a, f_b
     while 2 * left + 1 >= stride:
         low, high = halo - left, halo + slab - stride + left
-        low -= (high - low + 1) % 2
-
-        def pair_step(i, carry, low=low):
+        count, rest = (high - low + 1) // UNROLL, (high - low + 1) % UNROLL
+
+        def one(r, carry, old=old, new_f=new_f):
             row, flux = carry
-            for u in range(2):
-                r = low + 2 * i + u
-                above = stored(f, r + 1)
-                new, flux = row_update(row, above, flux, stored(fx, r), stored(fy, r), stored(fz, r), groups)
-                put(f, r, new)
-                row = above
-            return row, flux
-
-        row = stored(f, low)
-        below = stored(f, low - 1)
+            above = stored(old, r + 1)
+            new, flux = row_update(row, above, flux, stored(fx, r), stored(fy, r), stored(fz, r), groups)
+            put(new_f, r, new)
+            return above, flux
+
+        def several_steps(i, carry, low=low, one=one):
+            for u in range(UNROLL):
+                carry = one(low + UNROLL * i + u, carry)
+            return carry
+
+        row = stored(old, low)
+        below = stored(old, low - 1)
         face = stored(fx, low - 1)
         flux = [face[j] * (row[j] - below[j]) for j in range(groups)]
-        lax.fori_loop(0, (high - low + 1) // 2, pair_step, (row, flux))
+        carry = lax.fori_loop(0, count, several_steps, (row, flux))
+        for r in range(low + UNROLL * count, high + 1):
+            carry = one(r, carry)
+        old, new_f = new_f, old
         left -= 1
 
-    def cone(center, wanted, left):
-        def near(j, reach):
-            return any(min((j - w) % groups, (w - j) % groups) <= reach for w in wanted)
-
+    def cone_step(center, wanted, reach, old, new_f):
+        def near(j, far):
+            return any(min((j - w) % groups, (w - j) % groups) <= far for w in wanted)
+
+        flux = {}
+        for offset in range(-reach, reach + 1):
+            need = [j for j in range(groups) if near(j, reach - abs(offset))]
+            r = center + offset
+            cells = {}
+
+            def cell(j):
+                if j not in cells:
+                    cells[j] = old[r, j]
+                return cells[j]
+
+            below, flux, fluxes_y = flux, {}, {}
+
+            def flux_y(j):
+                if j not in fluxes_y:
+                    follow = cell(j + 1) if j + 1 < groups else pltpu.roll(cell(0), 7, 0)
+                    fluxes_y[j] = fy[r, j] * (follow - cell(j))
+                return fluxes_y[j]
+
+            for j in need:
+                here = cell(j)
+                flux[j] = fx[r, j] * (old[r + 1, j] - here)
+                lower = below[j] if j in below else fx[r - 1, j] * (here - old[r - 1, j])
+                before = flux_y(j - 1) if j else pltpu.roll(flux_y(groups - 1), 1, 0)
+                gz = fz[r, j] * (next_lane(here) - here)
+                new_f[r, j] = ((here + flux[j]) + (flux_y(j) + gz)) - ((lower + before) + last_lane(gz))
+
+    period = min(8, plan.rows)
+
+    def cones(i, _):
+        source, target = old, new_f
         for reach in range(left, -1, -1):
-            flux = {}
-            for offset in range(-reach, reach + 1):
-                need = [j for j in range(groups) if near(j, reach - abs(offset))]
-                r = center + offset
-                cells = {}
-
-                def cell(j):
-                    if j not in cells:
-                        cells[j] = f[r, j]
-                    return cells[j]
-
-                below, flux, fluxes_y, results = flux, {}, {}, {}
-
-                def flux_y(j):
-                    if j not in fluxes_y:
-                        follow = cell(j + 1) if j + 1 < groups else pltpu.roll(cell(0), 7, 0)
-                        fluxes_y[j] = fy[r, j] * (follow - cell(j))
-                    return fluxes_y[j]
-
-                for j in need:
-                    here = cell(j)
-                    flux[j] = fx[r, j] * (f[r + 1, j] - here)
-                    lower = below[j] if j in below else fx[r - 1, j] * (here - f[r - 1, j])
-                    before = flux_y(j - 1) if j else pltpu.roll(flux_y(groups - 1), 1, 0)
-                    gz = fz[r, j] * (next_lane(here) - here)
-                    results[j] = ((here + flux[j]) + (flux_y(j) + gz)) - ((lower + before) + last_lane(gz))
-                for j in need:
-                    f[r, j] = results[j]
-
-    period = min(4, plan.rows)
-
-    def cones(i, _):
-        for k in range(period):
-            spare = EXTRA - (0 if k == 0 else max(0, EXTRA - trailing_zeros(k)))
-            if k == 0 and period < 4:
-                spare = EXTRA
-            step = max(1, groups >> spare)
-            cone(halo + (i * period + k) * stride, list(range(0, groups, step)), left)
+            for k in range(period):
+                spare = EXTRA if k == 0 else min(EXTRA, trailing_zeros(k))
+                step = max(1, groups >> spare)
+                center = halo + (i * period + k) * stride
+                cone_step(center, list(range(0, groups, step)), reach, source, target)
+            source, target = target, source
         return 0
 
     lax.fori_loop(0, plan.rows // period, cones, 0)
+    done = old if left % 2 else new_f
 
     for k in range(plan.rows):
-        plane = f[halo + k * stride].reshape(groups * 8, LANES)
+        plane = done[halo + k * stride].reshape(groups * 8, LANES)
         out[k] = split_dot(split_dot(hy[...], plane, True), hz[...], False)
 
 
@@ -376,7 +386,7 @@
         out_shape=jax.ShapeDtypeStruct((plan.rows, kept, LANES), jnp.float32),
         in_specs=[anywhere, anywhere] + [vmem] * 6,
         out_specs=vmem,
-        scratch_shapes=[raw, raw, extended, extended, extended, extended, pltpu.SemaphoreType.DMA((2, slab // chunk))],
+        scratch_shapes=[raw, raw, extended, extended, extended, extended, extended, pltpu.SemaphoreType.DMA((2, slab // chunk))],
         compiler_params=params,
         name="diffuse",
     )(density, kappa, dprev, kprev, dnext, knext, hy, hz)

time: 129 us -> 97.4 us (0.76)
  Pallas kernels: 70.8 us -> 38.8 us
    pallas_call x1, Pallas kernels: 62.8 us -> 30.8 us  [local(): pl.pallas_call(functools.partial(diffuse_kernel, plan, slab, groups, chun...]
  transfers between devices with their start and end apart: 4 -> 4, of which waited for: 3 -> 3; matrix products, arithmetic and copies ran while one was open for 2% -> 3% of each run, Pallas kernels for 0% -> 0%
where the time goes in v2:
time: 97.4 us; the launch traced here: 96.9 us
  blocking collectives  45.7 us (47%)
  Pallas kernels  38.8 us (40%)
  local copies, waits for them, and re-layouts  4.92 us (5%)
  waiting for transfers between devices  3.56 us (4%)
  starting transfers between devices  3.19 us (3%)
    psum x1, blocking collectives, local(): packed = lax.psum(packed, 'grid')  39.4 us
    pallas_call x1, Pallas kernels, local(): pl.pallas_call(functools.partial(diffuse_kernel, plan, slab, groups, chun...  30.8 us
    all_gather x1, blocking collectives, local(): coarse = lax.all_gather(planes[0], 'space', axis=0)  6.37 us
    pallas_call x1, Pallas kernels, local(): pl.pallas_call(functools.partial(expand_kernel, plan, slab), out_shape=ja...  6.14 us
    ppermute x1, starting transfers between devices, local(): dprev = lax.ppermute(density[0, slab - ITERS:], 'space', up)  2.65 us
    ppermute x1, waiting for transfers between devices, local(): dprev = lax.ppermute(density[0, slab - ITERS:], 'space', up)  2.36 us
  transfers between devices with their start and end apart: 4, of which 3 were waited for; matrix products, arithmetic and copies ran while one was open for 3% of the time, Pallas kernels for 0%

profile of v2, /device:TPU:0, one launch (start us, length us, event | category | flops | bytes accessed | tf_op | source)
XLA Modules:
  0.0 96.9 jit_solution(2244798649491489547)
XLA Ops:
  0.0 1.0 slice_bitcast_fusion
  1.0 0.5 collective-permute-start.1
  1.5 1.0 slice_bitcast_fusion.1
  2.4 2.7 %collective-permute-start = (f32[8,64,128]{2,1,0:T(8,128)S(1)}, f32[8,64,128]{2,1,0:T(8,128)S(1)}, u32[]{:S(2)}, u32[]{:S(2)}) collective-permute-start(f32[8,64,128]{2,1,0:T(8,128)S(1)} %slice_bitcast_fusion.1), channel_id=1, source_target_pairs={{0,1},{1,2},{2,3},{3,0},{4,5},{5,6},{6,7},{7,4},{8,9},{9,10},{10,1... | collective-permute-start | bytes 786440 | tf_op jit(solution)/shard_map/ppermute | solution.py:371
  5.1 0.8 slice_bitcast_fusion.2
  5.9 0.0 collective-permute-start.3
  5.9 0.8 slice_bitcast_fusion.3
  6.6 0.0 collective-permute-start.2
  7.3 0.4 collective-permute-done.3.knext
  7.7 0.0 copy-start.2
  7.7 0.8 collective-permute-done.2.dnext
  8.5 0.0 copy-start.3
  8.5 0.0 collective-permute-done.1.kprev
  8.5 0.0 copy-start
  8.5 2.4 %collective-permute-done.dprev = f32[8,64,128]{2,1,0:T(8,128)S(1)} collective-permute-done((f32[8,64,128]{2,1,0:T(8,128)S(1)}, f32[8,64,128]{2,1,0:T(8,128)S(1)}, u32[]{:S(2)}, u32[]{:S(2)}) %collective-permute-start) | collective-permute-done | bytes 262176 | tf_op jit(solution)/shard_map/ppermute | solution.py:371
  10.9 0.0 copy-done.2
  10.9 0.0 copy-done.3
  10.9 0.0 copy-done
  10.9 0.0 copy-start.1
  10.9 0.7 copy-done.1
  11.6 30.8 %diffuse.1.planes = f32[16,64,128]{2,1,0:T(8,128)} custom-call(f32[1,128,64,128]{3,2,1,0:T(8,128)} %dens.1, f32[1,128,64,128]{3,2,1,0:T(8,128)} %kap.1, f32[8,64,128]{2,1,0:T(8,128)} %copy-done.1, f32[8,64,128]{2,1,0:T(8,128)} %copy-done, f32[1,64,128]{2,1,0:T(8,128)} %copy-done.3, f32[1,64,128]{2,1,0:T(8,128)} %copy-done.2, ...), custom_call_target="tpu_custom_call" | custom-call | tf_op jit(solution)/shard_map/diffuse/pallas_call | solution.py:384
  42.4 0.8 slice.20
  43.1 6.4 %all_gather.3.coarse = f32[4,64,128]{2,1,0:T(8,128)} all-gather(f32[1,64,128]{2,1,0:T(8,128)S(1)} %slice.20), channel_id=1, replica_groups=mesh['grid'=8,'space'=4] {'space'}, dimensions={0}, use_global_device_ids=true | all-gather | bytes 163840 | tf_op jit(solution)/shard_map/all_gather | solution.py:394
  49.5 1.9 %pack.1 = f32[9,8,128]{2,1,0:T(8,128)} custom-call(s32[1]{0:T(128)} %bitcast.pos_ref, s32[1,3]{1,0:T(1,128)} %levels.3, s32[1]{0:T(128)S(6)} %copy.11.coefs, s32[64,128]{1,0:T(8,128)} %constant.20.clone.ly, s32[64,128]{1,0:T(8,128)} %constant.21.clone.lz, f32[16,64,128]{2,1,0:T(8,128)} %diffuse.1.planes, f32[4,64,128]{2,1,0:T(8,128)} %all_gather.3.coarse), custom_call_target="tpu_custom_call" | custom-call | tf_op jit(solution)/shard_map/pack/pallas_call | solution.py:395
  51.4 39.4 %psum.7.packed = f32[9,8,128]{2,1,0:T(8,128)} all-reduce(f32[9,8,128]{2,1,0:T(8,128)} %pack.1), channel_id=1, replica_groups=mesh['grid'=8,'space'=4] {'grid'}, use_global_device_ids=true, to_apply=%region_0.0 | all-reduce | flops 9216 | bytes 73728 | tf_op jit(solution)/shard_map/psum | solution.py:404
  90.7 6.1 %expand.1 = f32[1,128,64,128]{3,2,1,0:T(8,128)} custom-call(s32[1]{0:T(128)} %bitcast.pos_ref, s32[1,3]{1,0:T(1,128)} %levels.3, s32[64,128]{1,0:T(8,128)} %constant.20.clone.ly, s32[64,128]{1,0:T(8,128)} %constant.21.clone.lz, bf16[64,64]{1,0:T(8,128)(2,1)} %constant.18.clone.dy, bf16[128,128]{1,0:T(8,128)(2,1)} %constant.19.clone.dz, f32[9,8,128]{2,1,0:T(8,128)} %psum.7.packed), custom_call_target="tpu_custom_call" | custom-call | tf_op jit(solution)/shard_map/expand/pallas_call | solution.py:406
Async XLA Ops:
  1.0 7.5 %collective-permute-start.1 = (f32[8,64,128]{2,1,0:T(8,128)S(1)}, f32[8,64,128]{2,1,0:T(8,128)S(1)}, u32[]{:S(2)}, u32[]{:S(2)}) collective-permute-start(f32[8,64,128]{2,1,0:T(8,128)S(1)} %slice_bitcast_fusion), channel_id=1, source_target_pairs={{0,1},{1,2},{2,3},{3,0},{4,5},{5,6},{6,7},{7,4},{8,9},{9,10},{10,1... | collective-permute-start | bytes 786440 | tf_op jit(solution)/shard_map/ppermute | solution.py:372
  2.4 8.4 %collective-permute-start = (f32[8,64,128]{2,1,0:T(8,128)S(1)}, f32[8,64,128]{2,1,0:T(8,128)S(1)}, u32[]{:S(2)}, u32[]{:S(2)}) collective-permute-start(f32[8,64,128]{2,1,0:T(8,128)S(1)} %slice_bitcast_fusion.1), channel_id=1, source_target_pairs={{0,1},{1,2},{2,3},{3,0},{4,5},{5,6},{6,7},{7,4},{8,9},{9,10},{10,1... | collective-permute-start | bytes 786440 | tf_op jit(solution)/shard_map/ppermute | solution.py:371
  5.9 1.9 %collective-permute-start.3 = (f32[1,64,128]{2,1,0:T(8,128)S(1)}, f32[1,64,128]{2,1,0:T(8,128)S(1)}, u32[]{:S(2)}, u32[]{:S(2)}) collective-permute-start(f32[1,64,128]{2,1,0:T(8,128)S(1)} %slice_bitcast_fusion.2), channel_id=1, source_target_pairs={{1,0},{2,1},{3,2},{0,3},{5,4},{6,5},{7,6},{4,7},{9,8},{10,9},{11,1... | collective-permute-start | bytes 98312 | tf_op jit(solution)/shard_map/ppermute | solution.py:374
  6.6 1.9 %collective-permute-start.2 = (f32[1,64,128]{2,1,0:T(8,128)S(1)}, f32[1,64,128]{2,1,0:T(8,128)S(1)}, u32[]{:S(2)}, u32[]{:S(2)}) collective-permute-start(f32[1,64,128]{2,1,0:T(8,128)S(1)} %slice_bitcast_fusion.3), channel_id=1, source_target_pairs={{1,0},{2,1},{3,2},{0,3},{5,4},{6,5},{7,6},{4,7},{9,8},{10,9},{11,1... | collective-permute-start | bytes 98312 | tf_op jit(solution)/shard_map/ppermute | solution.py:373
  7.7 3.2 %copy-start.2 = (f32[1,64,128]{2,1,0:T(8,128)}, f32[1,64,128]{2,1,0:T(8,128)S(1)}, u32[]{:S(2)}) copy-start(f32[1,64,128]{2,1,0:T(8,128)S(1)} %collective-permute-done.3.knext) | copy-start | bytes 98308
  8.5 2.4 %copy-start.3 = (f32[1,64,128]{2,1,0:T(8,128)}, f32[1,64,128]{2,1,0:T(8,128)S(1)}, u32[]{:S(2)}) copy-start(f32[1,64,128]{2,1,0:T(8,128)S(1)} %collective-permute-done.2.dnext) | copy-start | bytes 98308
  8.5 2.4 %copy-start = (f32[8,64,128]{2,1,0:T(8,128)}, f32[8,64,128]{2,1,0:T(8,128)S(1)}, u32[]{:S(2)}) copy-start(f32[8,64,128]{2,1,0:T(8,128)S(1)} %collective-permute-done.1.kprev) | copy-start | bytes 786436
  10.9 0.7 copy-start.1

commit v3 on v2

--- a/solution.py
+++ b/solution.py
@@ -271,23 +271,58 @@
     return (ly[...] <= levels[0, 1]) & (lz[...] <= levels[0, 2])
 
 
-def pack_kernel(plan, pos_ref, levels, coefs, ly, lz, planes, coarse, out):
+def combine_kernel(plan, grids, levels, coefs, ly, lz, planes, out, coarse, mine, pair, parts, send_sems, recv_sems):
+    members, rows = plan.members, plan.rows
+    here = lax.axis_index("space")
+    grid = lax.axis_index("grid")
+    partner = grid + 1 - 2 * lax.rem(grid, 2)
+    space_peers = [{"space": lax.rem(here + d, members)} for d in range(1, members)]
+    grid_peers = [{"grid": partner}] + [{"grid": lax.rem(grid + 2 * d, grids)} for d in range(1, grids // 2)]
+    peers = space_peers + grid_peers
+
+    barrier = pltpu.get_barrier_semaphore()
+    for peer in peers:
+        pl.semaphore_signal(barrier, inc=1, device_id=peer, device_id_type=pl.DeviceIdType.MESH)
+    pl.semaphore_wait(barrier, len(peers))
+
+    def remote(source, target, number):
+        return pltpu.make_async_remote_copy(
+            src_ref=source,
+            dst_ref=target,
+            send_sem=send_sems.at[number],
+            recv_sem=recv_sems.at[number],
+            device_id=peers[number],
+            device_id_type=pl.DeviceIdType.MESH,
+        )
+
+    gathers = [remote(planes.at[0], coarse.at[here], i) for i in range(members - 1)]
+    for copy in gathers:
+        copy.start()
+    coarse[here] = planes[0]
+
     mask = grid_mask(levels, ly, lz)
     weight = coefs[0].astype(jnp.float32)
-    members, rows = plan.members, plan.rows
+    fine = {}
+    for k in range(1, rows):
+        h = 1 << trailing_zeros(k)
+        fine[k] = planes[k] - 0.5 * planes[k - h]
+        if k + h < rows:
+            fine[k] = fine[k] - 0.5 * planes[k + h]
+    for copy in gathers:
+        copy.wait_recv()
     surplus = []
     for p in range(members):
-        if p == 0:
-            value = coarse[0]
-        else:
+        value = coarse[p]
+        if p:
             h = 1 << trailing_zeros(p)
-            value = coarse[p] - 0.5 * (coarse[p - h] + coarse[(p + h) % members])
+            value = value - 0.5 * (coarse[p - h] + coarse[(p + h) % members])
         surplus.append(value)
-    following = coarse[lax.rem(pos_ref[0] + 1, members)]
+    following = coarse[lax.rem(here + 1, members)]
     for k in range(1, rows):
-        h = 1 << trailing_zeros(k)
-        above = planes[k + h] if k + h < rows else following
-        surplus.append(planes[k] - 0.5 * (planes[k - h] + above))
+        value = fine[k]
+        if k + (1 << trailing_zeros(k)) == rows:
+            value = value - 0.5 * following
+        surplus.append(value)
     for row in range(len(surplus)):
         scale = jnp.where(plan.levels[row] <= levels[0, 0], weight, 0.0)
         surplus[row] = jnp.where(mask, scale * surplus[row], 0.0)
@@ -298,7 +333,22 @@
             piece = pltpu.roll(piece, lane, 1)
         tiles[tile] = piece if tiles[tile] is None else tiles[tile] + piece
     for tile in range(plan.tiles):
-        out[tile] = tiles[tile]
+        mine[tile] = tiles[tile]
+
+    swap = remote(mine, parts.at[0], members - 1)
+    swap.start()
+    swap.wait_recv()
+    pair[...] = mine[...] + parts[0]
+    spreads = [remote(pair, parts.at[i], members - 1 + i) for i in range(1, grids // 2)]
+    for copy in spreads:
+        copy.start()
+    total = pair[...]
+    for i, copy in enumerate(spreads):
+        copy.wait_recv()
+        total = total + parts[i + 1]
+    out[...] = total
+    for copy in gathers + [swap] + spreads:
+        copy.wait_send()
 
 
 def expand_kernel(plan, slab, pos_ref, levels, ly, lz, dy, dz, packed, out, coarse, nodes, buf, sems):
@@ -391,17 +441,25 @@
         name="diffuse",
     )(density, kappa, dprev, kprev, dnext, knext, hy, hz)
 
-    coarse = lax.all_gather(planes[0], "space", axis=0)
+    grids = lax.axis_size("grid")
+    peers = members - 1 + grids // 2
+    packed_shape = (plan.tiles, 8, LANES)
     packed = pl.pallas_call(
-        functools.partial(pack_kernel, plan),
-        out_shape=jax.ShapeDtypeStruct((plan.tiles, 8, LANES), jnp.float32),
-        in_specs=[smem, smem, smem] + [vmem] * 4,
+        functools.partial(combine_kernel, plan, grids),
+        out_shape=jax.ShapeDtypeStruct(packed_shape, jnp.float32),
+        in_specs=[smem, smem] + [vmem] * 3,
         out_specs=vmem,
-        compiler_params=params,
-        name="pack",
-    )(pos, levels, coefs, ly, lz, planes, coarse)
-
-    packed = lax.psum(packed, "grid")
+        scratch_shapes=[
+            pltpu.VMEM((members, kept, LANES), jnp.float32),
+            pltpu.VMEM(packed_shape, jnp.float32),
+            pltpu.VMEM(packed_shape, jnp.float32),
+            pltpu.VMEM((grids // 2,) + packed_shape, jnp.float32),
+            pltpu.SemaphoreType.DMA((peers,)),
+            pltpu.SemaphoreType.DMA((peers,)),
+        ],
+        compiler_params=pltpu.CompilerParams(vmem_limit_bytes=VMEM_LIMIT, collective_id=0, has_side_effects=True),
+        name="combine",
+    )(levels, coefs, ly, lz, planes)
 
     return pl.pallas_call(
         functools.partial(expand_kernel, plan, slab),

time: 97.4 us -> 65.8 us (0.68)
  blocking collectives: 45.7 us -> 0 us
  Pallas kernels: 38.8 us -> 53.8 us
    psum x1 -> x0, blocking collectives: 39.4 us -> none  [local(): packed = lax.psum(packed, 'grid')]
    pallas_call x1, Pallas kernels: 1.86 us -> 16.8 us  [local(): pl.pallas_call(functools.partial(combine_kernel, plan, grids), out_shape=...]
    all_gather x1 -> x0, blocking collectives: 6.37 us -> none  [local(): coarse = lax.all_gather(planes[0], 'space', axis=0)]
  transfers between devices with their start and end apart: 4 -> 4, of which waited for: 3 -> 3; matrix products, arithmetic and copies ran while one was open for 3% -> 4% of each run, Pallas kernels for 0% -> 0%
where the time goes in v3:
time: 65.8 us; the launch traced here: 65.4 us
  Pallas kernels  53.8 us (82%)
  local copies, waits for them, and re-layouts  4.16 us (6%)
  waiting for transfers between devices  3.56 us (5%)
  starting transfers between devices  3.19 us (5%)
  between operations  0.69 us (1%)
    pallas_call x1, Pallas kernels, local(): pl.pallas_call(functools.partial(diffuse_kernel, plan, slab, groups, chun...  30.8 us
    pallas_call x1, Pallas kernels, local(): pl.pallas_call(functools.partial(combine_kernel, plan, grids), out_shape=...  16.8 us
    pallas_call x1, Pallas kernels, local(): pl.pallas_call(functools.partial(expand_kernel, plan, slab), out_shape=ja...  6.14 us
    ppermute x1, starting transfers between devices, local(): dprev = lax.ppermute(density[0, slab - ITERS:], 'space', up)  2.65 us
    ppermute x1, waiting for transfers between devices, local(): dprev = lax.ppermute(density[0, slab - ITERS:], 'space', up)  2.36 us
  transfers between devices with their start and end apart: 4, of which 3 were waited for; matrix products, arithmetic and copies ran while one was open for 4% of the time, Pallas kernels for 0%

profile of v3, /device:TPU:0, one launch (start us, length us, event | category | flops | bytes accessed | tf_op | source)
XLA Modules:
  0.0 65.4 jit_solution(12759546163358891565)
XLA Ops:
  0.0 1.0 %slice_bitcast_fusion = f32[8,64,128]{2,1,0:T(8,128)S(1)} fusion(f32[1,128,64,128]{3,2,1,0:T(8,128)} %kap.1), kind=kLoop, calls=%fused_computation | loop fusion | bytes 524288 | tf_op jit(solution)/shard_map/squeeze | solution.py:422
  1.0 0.5 collective-permute-start.1
  1.5 1.0 %slice_bitcast_fusion.1 = f32[8,64,128]{2,1,0:T(8,128)S(1)} fusion(f32[1,128,64,128]{3,2,1,0:T(8,128)} %dens.1), kind=kLoop, calls=%fused_computation.1 | loop fusion | bytes 524288 | tf_op jit(solution)/shard_map/squeeze | solution.py:421
  2.4 2.7 %collective-permute-start = (f32[8,64,128]{2,1,0:T(8,128)S(1)}, f32[8,64,128]{2,1,0:T(8,128)S(1)}, u32[]{:S(2)}, u32[]{:S(2)}) collective-permute-start(f32[8,64,128]{2,1,0:T(8,128)S(1)} %slice_bitcast_fusion.1), channel_id=1, source_target_pairs={{0,1},{1,2},{2,3},{3,0},{4,5},{5,6},{6,7},{7,4},{8,9},{9,10},{10,1... | collective-permute-start | bytes 786440 | tf_op jit(solution)/shard_map/ppermute | solution.py:421
  5.1 0.8 %slice_bitcast_fusion.2 = f32[1,64,128]{2,1,0:T(8,128)S(1)} fusion(f32[1,128,64,128]{3,2,1,0:T(8,128)} %kap.1), kind=kLoop, calls=%fused_computation.2 | loop fusion | bytes 65536 | tf_op jit(solution)/shard_map/squeeze | solution.py:424
  5.9 0.0 collective-permute-start.3
  5.9 0.8 %slice_bitcast_fusion.3 = f32[1,64,128]{2,1,0:T(8,128)S(1)} fusion(f32[1,128,64,128]{3,2,1,0:T(8,128)} %dens.1), kind=kLoop, calls=%fused_computation.3 | loop fusion | bytes 65536 | tf_op jit(solution)/shard_map/squeeze | solution.py:423
  6.6 0.0 collective-permute-start.2
  7.3 0.4 collective-permute-done.3.knext
  7.7 0.0 copy-start.2
  7.7 0.8 %collective-permute-done.2.dnext = f32[1,64,128]{2,1,0:T(8,128)S(1)} collective-permute-done((f32[1,64,128]{2,1,0:T(8,128)S(1)}, f32[1,64,128]{2,1,0:T(8,128)S(1)}, u32[]{:S(2)}, u32[]{:S(2)}) %collective-permute-start.2) | collective-permute-done | bytes 32800 | tf_op jit(solution)/shard_map/ppermute | solution.py:423
  8.5 0.0 copy-start.3
  8.5 0.0 collective-permute-done.1.kprev
  8.5 0.0 copy-start
  8.5 2.4 %collective-permute-done.dprev = f32[8,64,128]{2,1,0:T(8,128)S(1)} collective-permute-done((f32[8,64,128]{2,1,0:T(8,128)S(1)}, f32[8,64,128]{2,1,0:T(8,128)S(1)}, u32[]{:S(2)}, u32[]{:S(2)}) %collective-permute-start) | collective-permute-done | bytes 262176 | tf_op jit(solution)/shard_map/ppermute | solution.py:421
  10.9 0.0 copy-done.2
  10.9 0.0 copy-done.3
  10.9 0.0 copy-done
  10.9 0.0 copy-start.1
  10.9 0.7 %copy-done.1 = f32[8,64,128]{2,1,0:T(8,128)} copy-done((f32[8,64,128]{2,1,0:T(8,128)}, f32[8,64,128]{2,1,0:T(8,128)S(1)}, u32[]{:S(2)}) %copy-start.1) | copy-done | bytes 262168
  11.6 30.8 %diffuse.1.planes = f32[16,64,128]{2,1,0:T(8,128)} custom-call(f32[1,128,64,128]{3,2,1,0:T(8,128)} %dens.1, f32[1,128,64,128]{3,2,1,0:T(8,128)} %kap.1, f32[8,64,128]{2,1,0:T(8,128)} %copy-done.1, f32[8,64,128]{2,1,0:T(8,128)} %copy-done, f32[1,64,128]{2,1,0:T(8,128)} %copy-done.3, f32[1,64,128]{2,1,0:T(8,128)} %copy-done.2, ...), custom_call_target="tpu_custom_call" | custom-call | tf_op jit(solution)/shard_map/diffuse/pallas_call | solution.py:434
  42.4 16.8 %combine.1.packed = f32[9,8,128]{2,1,0:T(8,128)} custom-call(s32[1,3]{1,0:T(1,128)} %levels.3, s32[1]{0:T(128)S(6)} %copy.11.coefs, s32[64,128]{1,0:T(8,128)} %constant.20.clone.ly, s32[64,128]{1,0:T(8,128)} %constant.21.clone.lz, f32[16,64,128]{2,1,0:T(8,128)} %diffuse.1.planes), custom_call_target="tpu_custom_call" | custom-call | tf_op jit(solution)/shard_map/combine/pallas_call | solution.py:447
  59.2 6.1 %expand.1 = f32[1,128,64,128]{3,2,1,0:T(8,128)} custom-call(s32[1]{0:T(128)} %bitcast.pos_ref, s32[1,3]{1,0:T(1,128)} %levels.3, s32[64,128]{1,0:T(8,128)} %constant.20.clone.ly, s32[64,128]{1,0:T(8,128)} %constant.21.clone.lz, bf16[64,64]{1,0:T(8,128)(2,1)} %constant.18.clone.dy, bf16[128,128]{1,0:T(8,128)(2,1)} %constant.19.clone.dz, ...), custom_call_target="tpu_custom_call" | custom-call | tf_op jit(solution)/shard_map/expand/pallas_call | solution.py:464
Async XLA Ops:
  1.0 7.5 %collective-permute-start.1 = (f32[8,64,128]{2,1,0:T(8,128)S(1)}, f32[8,64,128]{2,1,0:T(8,128)S(1)}, u32[]{:S(2)}, u32[]{:S(2)}) collective-permute-start(f32[8,64,128]{2,1,0:T(8,128)S(1)} %slice_bitcast_fusion), channel_id=1, source_target_pairs={{0,1},{1,2},{2,3},{3,0},{4,5},{5,6},{6,7},{7,4},{8,9},{9,10},{10,1... | collective-permute-start | bytes 786440 | tf_op jit(solution)/shard_map/ppermute | solution.py:422
  2.4 8.4 %collective-permute-start = (f32[8,64,128]{2,1,0:T(8,128)S(1)}, f32[8,64,128]{2,1,0:T(8,128)S(1)}, u32[]{:S(2)}, u32[]{:S(2)}) collective-permute-start(f32[8,64,128]{2,1,0:T(8,128)S(1)} %slice_bitcast_fusion.1), channel_id=1, source_target_pairs={{0,1},{1,2},{2,3},{3,0},{4,5},{5,6},{6,7},{7,4},{8,9},{9,10},{10,1... | collective-permute-start | bytes 786440 | tf_op jit(solution)/shard_map/ppermute | solution.py:421
  5.9 1.9 %collective-permute-start.3 = (f32[1,64,128]{2,1,0:T(8,128)S(1)}, f32[1,64,128]{2,1,0:T(8,128)S(1)}, u32[]{:S(2)}, u32[]{:S(2)}) collective-permute-start(f32[1,64,128]{2,1,0:T(8,128)S(1)} %slice_bitcast_fusion.2), channel_id=1, source_target_pairs={{1,0},{2,1},{3,2},{0,3},{5,4},{6,5},{7,6},{4,7},{9,8},{10,9},{11,1... | collective-permute-start | bytes 98312 | tf_op jit(solution)/shard_map/ppermute | solution.py:424
  6.6 1.9 %collective-permute-start.2 = (f32[1,64,128]{2,1,0:T(8,128)S(1)}, f32[1,64,128]{2,1,0:T(8,128)S(1)}, u32[]{:S(2)}, u32[]{:S(2)}) collective-permute-start(f32[1,64,128]{2,1,0:T(8,128)S(1)} %slice_bitcast_fusion.3), channel_id=1, source_target_pairs={{1,0},{2,1},{3,2},{0,3},{5,4},{6,5},{7,6},{4,7},{9,8},{10,9},{11,1... | collective-permute-start | bytes 98312 | tf_op jit(solution)/shard_map/ppermute | solution.py:423
  7.7 3.2 %copy-start.2 = (f32[1,64,128]{2,1,0:T(8,128)}, f32[1,64,128]{2,1,0:T(8,128)S(1)}, u32[]{:S(2)}) copy-start(f32[1,64,128]{2,1,0:T(8,128)S(1)} %collective-permute-done.3.knext) | copy-start | bytes 98308
  8.5 2.4 %copy-start.3 = (f32[1,64,128]{2,1,0:T(8,128)}, f32[1,64,128]{2,1,0:T(8,128)S(1)}, u32[]{:S(2)}) copy-start(f32[1,64,128]{2,1,0:T(8,128)S(1)} %collective-permute-done.2.dnext) | copy-start | bytes 98308
  8.5 2.4 %copy-start = (f32[8,64,128]{2,1,0:T(8,128)}, f32[8,64,128]{2,1,0:T(8,128)S(1)}, u32[]{:S(2)}) copy-start(f32[8,64,128]{2,1,0:T(8,128)S(1)} %collective-permute-done.1.kprev) | copy-start | bytes 786436
  10.9 0.7 %copy-start.1 = (f32[8,64,128]{2,1,0:T(8,128)}, f32[8,64,128]{2,1,0:T(8,128)S(1)}, u32[]{:S(2)}) copy-start(f32[8,64,128]{2,1,0:T(8,128)S(1)} %collective-permute-done.dprev) | copy-start | bytes 786436

commit v4 on v3

--- a/solution.py
+++ b/solution.py
@@ -111,28 +111,29 @@
 
 
 def next_lane(v):
-    return pltpu.roll(v, LANES - 1, 1)
+    return pltpu.roll(v, LANES - 1, v.ndim - 1)
 
 
 def last_lane(v):
-    return pltpu.roll(v, 1, 1)
-
-
-def row_update(f, above, flux_below, fx, fy, fz, groups):
-    gx = [fx[j] * (above[j] - f[j]) for j in range(groups)]
-    follow = f[1:] + [pltpu.roll(f[0], 7, 0)]
-    gy = [fy[j] * (follow[j] - f[j]) for j in range(groups)]
-    before = [pltpu.roll(gy[-1], 1, 0)] + gy[:-1]
-    new = []
-    for j in range(groups):
-        gz = fz[j] * (next_lane(f[j]) - f[j])
-        plus = (f[j] + gx[j]) + (gy[j] + gz)
-        minus = (flux_below[j] + before[j]) + last_lane(gz)
-        new.append(plus - minus)
-    return new, gx
-
-
-def diffuse_kernel(plan, slab, groups, chunk, dens, kap, dprev, kprev, dnext, knext, hy, hz, out, raw_d, raw_k, f_a, f_b, fx, fy, fz, sems):
+    return pltpu.roll(v, 1, v.ndim - 1)
+
+
+def next_y(v):
+    return jnp.concatenate([v[1:], pltpu.roll(v[:1], 7, 1)], axis=0)
+
+
+def last_y(v):
+    return jnp.concatenate([pltpu.roll(v[-1:], 1, 1), v[:-1]], axis=0)
+
+
+def row_update(f, above, flux_below, fx, fy, fz):
+    gx = fx * (above - f)
+    gy = fy * (next_y(f) - f)
+    gz = fz * (next_lane(f) - f)
+    return ((f + gx) + (gy + gz)) - ((flux_below + last_y(gy)) + last_lane(gz)), gx
+
+
+def diffuse_kernel(plan, slab, groups, chunk, dens, kap, hy, hz, out, raw_d, raw_k, dprev, kprev, dnext, knext, f_a, f_b, fx, fy, fz, sems, send_sems, recv_sems):
     halo = ITERS
     chunks = slab // chunk
     copies = []
@@ -146,45 +147,76 @@
             copy.start()
         copies.append(pair)
 
+    here = lax.axis_index("space")
+    up = {"space": lax.rem(here + 1, plan.members)}
+    down = {"space": lax.rem(here + plan.members - 1, plan.members)}
+    barrier = pltpu.get_barrier_semaphore()
+    for peer in (up, down):
+        pl.semaphore_signal(barrier, inc=1, device_id=peer, device_id_type=pl.DeviceIdType.MESH)
+    pl.semaphore_wait(barrier, 2)
+    last, initial = pl.ds(slab - halo, halo), pl.ds(0, 1)
+    sends = []
+    for i, (source, target, peer) in enumerate(
+        (
+            (kap.at[0, last], kprev, up),
+            (dens.at[0, last], dprev, up),
+            (kap.at[0, initial], knext, down),
+            (dens.at[0, initial], dnext, down),
+        )
+    ):
+        copy = pltpu.make_async_remote_copy(
+            src_ref=source,
+            dst_ref=target,
+            send_sem=send_sems.at[i],
+            recv_sem=recv_sems.at[i],
+            device_id=peer,
+            device_id_type=pl.DeviceIdType.MESH,
+        )
+        copy.start()
+        sends.append(copy)
+
     def natural(ref, row):
-        return [ref[row, pl.ds(j, 8, stride=groups), :] for j in range(groups)]
-
-    def stored(ref, row):
-        return [ref[row, j] for j in range(groups)]
-
-    def put(ref, row, values):
-        for j in range(groups):
-            ref[row, j] = values[j]
+        return jnp.stack([ref[row, pl.ds(j, 8, stride=groups), :] for j in range(groups)], axis=0)
 
     def first(r, k_above, d_above, carry):
         k, d, flux = carry
-        x_face = [0.5 * (k[j] + k_above[j]) for j in range(groups)]
-        k_next = k[1:] + [pltpu.roll(k[0], 7, 0)]
-        y_face = [0.5 * (k[j] + k_next[j]) for j in range(groups)]
-        z_face = [0.5 * (k[j] + next_lane(k[j])) for j in range(groups)]
-        put(fx, r - 1, x_face)
-        put(fy, r - 1, y_face)
-        put(fz, r - 1, z_face)
-        new, flux = row_update(d, d_above, flux, x_face, y_face, z_face, groups)
-        put(f_a, r - 1, new)
+        x_face = 0.5 * (k + k_above)
+        y_face = 0.5 * (k + next_y(k))
+        z_face = 0.5 * (k + next_lane(k))
+        fx[r - 1] = x_face
+        fy[r - 1] = y_face
+        fz[r - 1] = z_face
+        f_a[r - 1], flux = row_update(d, d_above, flux, x_face, y_face, z_face)
         return k_above, d_above, flux
 
-    zero = [jnp.zeros((8, LANES), jnp.float32)] * groups
+    def both(x, carry):
+        return first(x + halo, natural(raw_k, x), natural(raw_d, x), carry)
+
+    zero = jnp.zeros((groups, 8, LANES), jnp.float32)
+    for c in range(chunks):
+        for copy in copies[c]:
+            copy.wait()
+        start, rest = c * chunk, chunk
+        if c == 0:
+            carry = (natural(raw_k, 0), natural(raw_d, 0), zero)
+            start, rest = 1, chunk - 1
+
+        def several(i, carry, start=start):
+            for u in range(UNROLL):
+                carry = both(start + i * UNROLL + u, carry)
+            return carry
+
+        carry = lax.fori_loop(0, rest // UNROLL, several, carry)
+        for x in range(start + rest // UNROLL * UNROLL, start + rest):
+            carry = both(x, carry)
+    for copy in sends:
+        copy.wait_recv()
+    first(slab + halo, natural(knext, 0), natural(dnext, 0), carry)
     carry = (natural(kprev, 0), natural(dprev, 0), zero)
     for r in range(1, halo):
         carry = first(r, natural(kprev, r), natural(dprev, r), carry)
-    for c in range(chunks):
-        for copy in copies[c]:
-            copy.wait()
-
-        def several(i, carry, c=c):
-            for u in range(UNROLL):
-                x = c * chunk + i * UNROLL + u
-                carry = first(x + halo, natural(raw_k, x), natural(raw_d, x), carry)
-            return carry
-
-        carry = lax.fori_loop(0, chunk // UNROLL, several, carry)
-    first(slab + halo, natural(knext, 0), natural(dnext, 0), carry)
+    carry = both(0, carry)
+    f_a[halo] = f_a[halo] - carry[2]
 
     stride = plan.stride
     left = ITERS - 2
@@ -195,9 +227,8 @@
 
         def one(r, carry, old=old, new_f=new_f):
             row, flux = carry
-            above = stored(old, r + 1)
-            new, flux = row_update(row, above, flux, stored(fx, r), stored(fy, r), stored(fz, r), groups)
-            put(new_f, r, new)
+            above = old[r + 1]
+            new_f[r], flux = row_update(row, above, flux, fx[r], fy[r], fz[r])
             return above, flux
 
         def several_steps(i, carry, low=low, one=one):
@@ -205,10 +236,8 @@
                 carry = one(low + UNROLL * i + u, carry)
             return carry
 
-        row = stored(old, low)
-        below = stored(old, low - 1)
-        face = stored(fx, low - 1)
-        flux = [face[j] * (row[j] - below[j]) for j in range(groups)]
+        row = old[low]
+        flux = fx[low - 1] * (row - old[low - 1])
         carry = lax.fori_loop(0, count, several_steps, (row, flux))
         for r in range(low + UNROLL * count, high + 1):
             carry = one(r, carry)
@@ -262,9 +291,14 @@
     lax.fori_loop(0, plan.rows // period, cones, 0)
     done = old if left % 2 else new_f
 
+    planes = [done[halo + k * stride].reshape(groups * 8, LANES) for k in range(plan.rows)]
+    planes = split_dot(jnp.concatenate(planes, axis=0), hz[...], False)
+    planes = jnp.concatenate([planes[k * groups * 8 : (k + 1) * groups * 8] for k in range(plan.rows)], axis=1)
+    planes = split_dot(hy[...], planes, True)
     for k in range(plan.rows):
-        plane = done[halo + k * stride].reshape(groups * 8, LANES)
-        out[k] = split_dot(split_dot(hy[...], plane, True), hz[...], False)
+        out[k] = planes[:, k * LANES : (k + 1) * LANES]
+    for copy in sends:
+        copy.wait_send()
 
 
 def grid_mask(levels, ly, lz):
@@ -385,8 +419,6 @@
         for k in range(h, rows, 2 * h):
             fine[k] = fine[k] + 0.5 * (fine[k - h] + fine[k + h])
         h //= 2
-    for k in range(rows + 1):
-        nodes[k] = split_dot(dy[...], split_dot(fine[k], dz[...], False), True)
 
     def chunk(k):
         part = pl.ds(k * stride, stride)
@@ -400,7 +432,19 @@
         chunk(k).start()
         return 0
 
-    lax.fori_loop(0, rows, fill, 0)
+    def transform(low, high):
+        size = fine[0].shape[0]
+        part = split_dot(jnp.concatenate(fine[low:high], axis=0), dz[...], False)
+        part = jnp.concatenate([part[i * size : (i + 1) * size] for i in range(high - low)], axis=1)
+        part = split_dot(dy[...], part, True)
+        for i in range(high - low):
+            nodes[low + i] = part[:, i * LANES : (i + 1) * LANES]
+
+    half = rows // 2
+    transform(0, half + 1)
+    lax.fori_loop(0, half, fill, 0)
+    transform(half + 1, rows + 1)
+    lax.fori_loop(half, rows, fill, 0)
 
     def drain(k, _):
         chunk(k).wait()
@@ -416,13 +460,6 @@
     position = lax.axis_index("space")
     hy, hz, dy, dz, ly, lz = axis_tables(width_y, width_z)
     pos = jnp.reshape(position, (1,)).astype(jnp.int32)
-    up = [(i, (i + 1) % members) for i in range(members)]
-    down = [(j, i) for i, j in up]
-    dprev = lax.ppermute(density[0, slab - ITERS :], "space", up)
-    kprev = lax.ppermute(kappa[0, slab - ITERS :], "space", up)
-    dnext = lax.ppermute(density[0, :1], "space", down)
-    knext = lax.ppermute(kappa[0, :1], "space", down)
-
     vmem = pl.BlockSpec(memory_space=pltpu.VMEM)
     smem = pl.BlockSpec(memory_space=pltpu.SMEM)
     anywhere = pl.BlockSpec(memory_space=pl.ANY)
@@ -431,15 +468,19 @@
     chunk = min(32, slab)
     extended = pltpu.VMEM((slab + ITERS, groups, 8, LANES), jnp.float32)
     raw = pltpu.VMEM((slab, width_y, width_z), jnp.float32)
+    below = pltpu.VMEM((ITERS, width_y, width_z), jnp.float32)
+    above = pltpu.VMEM((1, width_y, width_z), jnp.float32)
     planes = pl.pallas_call(
         functools.partial(diffuse_kernel, plan, slab, groups, chunk),
         out_shape=jax.ShapeDtypeStruct((plan.rows, kept, LANES), jnp.float32),
-        in_specs=[anywhere, anywhere] + [vmem] * 6,
+        in_specs=[anywhere, anywhere, vmem, vmem],
         out_specs=vmem,
-        scratch_shapes=[raw, raw, extended, extended, extended, extended, extended, pltpu.SemaphoreType.DMA((2, slab // chunk))],
-        compiler_params=params,
+        scratch_shapes=[raw, raw, below, below, above, above]
+        + [extended] * 5
+        + [pltpu.SemaphoreType.DMA((2, slab // chunk)), pltpu.SemaphoreType.DMA((4,)), pltpu.SemaphoreType.DMA((4,))],
+        compiler_params=pltpu.CompilerParams(vmem_limit_bytes=VMEM_LIMIT, collective_id=1, has_side_effects=True),
         name="diffuse",
-    )(density, kappa, dprev, kprev, dnext, knext, hy, hz)
+    )(density, kappa, hy, hz)
 
     grids = lax.axis_size("grid")
     peers = members - 1 + grids // 2

time: 65.8 us -> 50.7 us (0.77)
  local copies, waits for them, and re-layouts: 4.16 us -> 0 us
  Pallas kernels: 53.8 us -> 49.7 us
  waiting for transfers between devices: 3.56 us -> 0 us
  starting transfers between devices: 3.19 us -> 0 us
    ppermute x4 -> x0, waiting for transfers between devices: 3.56 us -> none  [the longest x1 2.36 us: local(): dprev = lax.ppermute(density[0, slab - ITERS:], 'space', up)]
    squeeze x4 -> x0, local copies, waits for them, and re-layouts: 3.46 us -> none  [the longest x1 0.97 us: local(): dprev = lax.ppermute(density[0, slab - ITERS:], 'space', up)]
    ppermute x4 -> x0, starting transfers between devices: 3.19 us -> none  [the longest x1 2.65 us: local(): dprev = lax.ppermute(density[0, slab - ITERS:], 'space', up)]
    pallas_call x1, Pallas kernels: 6.14 us -> 3.62 us  [local(): pl.pallas_call(functools.partial(expand_kernel, plan, slab), out_shape=ja...]
    pallas_call x1, Pallas kernels: 16.8 us -> 16.1 us  [local(): pl.pallas_call(functools.partial(combine_kernel, plan, grids), out_shape=...]
    pallas_call x1, Pallas kernels: 30.8 us -> 30 us  [local(): pl.pallas_call(functools.partial(diffuse_kernel, plan, slab, groups, chun...]
    unnamed x8 -> x0, local copies, waits for them, and re-layouts: 0.7 us -> none
  transfers between devices with their start and end apart: 4 -> 0, of which waited for: 3 -> 0; matrix products, arithmetic and copies ran while one was open for 4% -> 0% of each run, Pallas kernels for 0% -> 0%
where the time goes in v4:
time: 50.7 us; the launch traced here: 50.4 us
  Pallas kernels  49.7 us (98%)
  between operations  0.67 us (1%)
    pallas_call x1, Pallas kernels, local(): pl.pallas_call(functools.partial(diffuse_kernel, plan, slab, groups, chun...  30 us
    pallas_call x1, Pallas kernels, local(): pl.pallas_call(functools.partial(combine_kernel, plan, grids), out_shape=...  16.1 us
    pallas_call x1, Pallas kernels, local(): pl.pallas_call(functools.partial(expand_kernel, plan, slab), out_shape=ja...  3.62 us

profile of v4, /device:TPU:0, one launch (start us, length us, event | category | flops | bytes accessed | tf_op | source)
XLA Modules:
  0.0 50.4 jit_solution(16865027697534041220)
XLA Ops:
  0.7 30.0 %diffuse.1.planes = f32[16,64,128]{2,1,0:T(8,128)} custom-call(f32[1,128,64,128]{3,2,1,0:T(8,128)} %dens.1, f32[1,128,64,128]{3,2,1,0:T(8,128)} %kap.1, bf16[64,64]{1,0:T(8,128)(2,1)} %constant.16.clone.hy, bf16[128,128]{1,0:T(8,128)(2,1)} %constant.17.clone.hz), custom_call_target="tpu_custom_call" | custom-call | tf_op jit(solution)/shard_map/diffuse/pallas_call | solution.py:473
  30.7 16.1 %combine.1.packed = f32[9,8,128]{2,1,0:T(8,128)} custom-call(s32[1,3]{1,0:T(1,128)} %levels.3, s32[1]{0:T(128)S(6)} %copy.11.coefs, s32[64,128]{1,0:T(8,128)} %constant.20.clone.ly, s32[64,128]{1,0:T(8,128)} %constant.21.clone.lz, f32[16,64,128]{2,1,0:T(8,128)} %diffuse.1.planes), custom_call_target="tpu_custom_call" | custom-call | tf_op jit(solution)/shard_map/combine/pallas_call | solution.py:488
  46.8 3.6 %expand.1 = f32[1,128,64,128]{3,2,1,0:T(8,128)} custom-call(s32[1]{0:T(128)} %bitcast.pos_ref, s32[1,3]{1,0:T(1,128)} %levels.3, s32[64,128]{1,0:T(8,128)} %constant.20.clone.ly, s32[64,128]{1,0:T(8,128)} %constant.21.clone.lz, bf16[64,64]{1,0:T(8,128)(2,1)} %constant.18.clone.dy, bf16[128,128]{1,0:T(8,128)(2,1)} %constant.19.clone.dz, ...), custom_call_target="tpu_custom_call" | custom-call | tf_op jit(solution)/shard_map/expand/pallas_call | solution.py:505

commit v5 on v4

--- a/solution.py
+++ b/solution.py
@@ -13,7 +13,7 @@
 EXTRA = 3
 TOP = BASE + EXTRA
 LANES = 128
-UNROLL = 8
+UNROLL = 16
 VMEM_LIMIT = 56 * 1024 * 1024
 
 
@@ -133,207 +133,12 @@
     return ((f + gx) + (gy + gz)) - ((flux_below + last_y(gy)) + last_lane(gz)), gx
 
 
-def diffuse_kernel(plan, slab, groups, chunk, dens, kap, hy, hz, out, raw_d, raw_k, dprev, kprev, dnext, knext, f_a, f_b, fx, fy, fz, sems, send_sems, recv_sems):
-    halo = ITERS
-    chunks = slab // chunk
-    copies = []
-    for c in range(chunks):
-        part = pl.ds(c * chunk, chunk)
-        pair = (
-            pltpu.make_async_copy(kap.at[0, part], raw_k.at[part], sems.at[0, c]),
-            pltpu.make_async_copy(dens.at[0, part], raw_d.at[part], sems.at[1, c]),
-        )
-        for copy in pair:
-            copy.start()
-        copies.append(pair)
-
-    here = lax.axis_index("space")
-    up = {"space": lax.rem(here + 1, plan.members)}
-    down = {"space": lax.rem(here + plan.members - 1, plan.members)}
-    barrier = pltpu.get_barrier_semaphore()
-    for peer in (up, down):
-        pl.semaphore_signal(barrier, inc=1, device_id=peer, device_id_type=pl.DeviceIdType.MESH)
-    pl.semaphore_wait(barrier, 2)
-    last, initial = pl.ds(slab - halo, halo), pl.ds(0, 1)
-    sends = []
-    for i, (source, target, peer) in enumerate(
-        (
-            (kap.at[0, last], kprev, up),
-            (dens.at[0, last], dprev, up),
-            (kap.at[0, initial], knext, down),
-            (dens.at[0, initial], dnext, down),
-        )
-    ):
-        copy = pltpu.make_async_remote_copy(
-            src_ref=source,
-            dst_ref=target,
-            send_sem=send_sems.at[i],
-            recv_sem=recv_sems.at[i],
-            device_id=peer,
-            device_id_type=pl.DeviceIdType.MESH,
-        )
-        copy.start()
-        sends.append(copy)
-
-    def natural(ref, row):
-        return jnp.stack([ref[row, pl.ds(j, 8, stride=groups), :] for j in range(groups)], axis=0)
-
-    def first(r, k_above, d_above, carry):
-        k, d, flux = carry
-        x_face = 0.5 * (k + k_above)
-        y_face = 0.5 * (k + next_y(k))
-        z_face = 0.5 * (k + next_lane(k))
-        fx[r - 1] = x_face
-        fy[r - 1] = y_face
-        fz[r - 1] = z_face
-        f_a[r - 1], flux = row_update(d, d_above, flux, x_face, y_face, z_face)
-        return k_above, d_above, flux
-
-    def both(x, carry):
-        return first(x + halo, natural(raw_k, x), natural(raw_d, x), carry)
-
-    zero = jnp.zeros((groups, 8, LANES), jnp.float32)
-    for c in range(chunks):
-        for copy in copies[c]:
-            copy.wait()
-        start, rest = c * chunk, chunk
-        if c == 0:
-            carry = (natural(raw_k, 0), natural(raw_d, 0), zero)
-            start, rest = 1, chunk - 1
-
-        def several(i, carry, start=start):
-            for u in range(UNROLL):
-                carry = both(start + i * UNROLL + u, carry)
-            return carry
-
-        carry = lax.fori_loop(0, rest // UNROLL, several, carry)
-        for x in range(start + rest // UNROLL * UNROLL, start + rest):
-            carry = both(x, carry)
-    for copy in sends:
-        copy.wait_recv()
-    first(slab + halo, natural(knext, 0), natural(dnext, 0), carry)
-    carry = (natural(kprev, 0), natural(dprev, 0), zero)
-    for r in range(1, halo):
-        carry = first(r, natural(kprev, r), natural(dprev, r), carry)
-    carry = both(0, carry)
-    f_a[halo] = f_a[halo] - carry[2]
-
-    stride = plan.stride
-    left = ITERS - 2
-    old, new_f = f_a, f_b
-    while 2 * left + 1 >= stride:
-        low, high = halo - left, halo + slab - stride + left
-        count, rest = (high - low + 1) // UNROLL, (high - low + 1) % UNROLL
-
-        def one(r, carry, old=old, new_f=new_f):
-            row, flux = carry
-            above = old[r + 1]
-            new_f[r], flux = row_update(row, above, flux, fx[r], fy[r], fz[r])
-            return above, flux
-
-        def several_steps(i, carry, low=low, one=one):
-            for u in range(UNROLL):
-                carry = one(low + UNROLL * i + u, carry)
-            return carry
-
-        row = old[low]
-        flux = fx[low - 1] * (row - old[low - 1])
-        carry = lax.fori_loop(0, count, several_steps, (row, flux))
-        for r in range(low + UNROLL * count, high + 1):
-            carry = one(r, carry)
-        old, new_f = new_f, old
-        left -= 1
-
-    def cone_step(center, wanted, reach, old, new_f):
-        def near(j, far):
-            return any(min((j - w) % groups, (w - j) % groups) <= far for w in wanted)
-
-        flux = {}
-        for offset in range(-reach, reach + 1):
-            need = [j for j in range(groups) if near(j, reach - abs(offset))]
-            r = center + offset
-            cells = {}
-
-            def cell(j):
-                if j not in cells:
-                    cells[j] = old[r, j]
-                return cells[j]
-
-            below, flux, fluxes_y = flux, {}, {}
-
-            def flux_y(j):
-                if j not in fluxes_y:
-                    follow = cell(j + 1) if j + 1 < groups else pltpu.roll(cell(0), 7, 0)
-                    fluxes_y[j] = fy[r, j] * (follow - cell(j))
-                return fluxes_y[j]
-
-            for j in need:
-                here = cell(j)
-                flux[j] = fx[r, j] * (old[r + 1, j] - here)
-                lower = below[j] if j in below else fx[r - 1, j] * (here - old[r - 1, j])
-                before = flux_y(j - 1) if j else pltpu.roll(flux_y(groups - 1), 1, 0)
-                gz = fz[r, j] * (next_lane(here) - here)
-                new_f[r, j] = ((here + flux[j]) + (flux_y(j) + gz)) - ((lower + before) + last_lane(gz))
-
-    period = min(8, plan.rows)
-
-    def cones(i, _):
-        source, target = old, new_f
-        for reach in range(left, -1, -1):
-            for k in range(period):
-                spare = EXTRA if k == 0 else min(EXTRA, trailing_zeros(k))
-                step = max(1, groups >> spare)
-                center = halo + (i * period + k) * stride
-                cone_step(center, list(range(0, groups, step)), reach, source, target)
-            source, target = target, source
-        return 0
-
-    lax.fori_loop(0, plan.rows // period, cones, 0)
-    done = old if left % 2 else new_f
-
-    planes = [done[halo + k * stride].reshape(groups * 8, LANES) for k in range(plan.rows)]
-    planes = split_dot(jnp.concatenate(planes, axis=0), hz[...], False)
-    planes = jnp.concatenate([planes[k * groups * 8 : (k + 1) * groups * 8] for k in range(plan.rows)], axis=1)
-    planes = split_dot(hy[...], planes, True)
-    for k in range(plan.rows):
-        out[k] = planes[:, k * LANES : (k + 1) * LANES]
-    for copy in sends:
-        copy.wait_send()
-
-
 def grid_mask(levels, ly, lz):
     return (ly[...] <= levels[0, 1]) & (lz[...] <= levels[0, 2])
 
 
-def combine_kernel(plan, grids, levels, coefs, ly, lz, planes, out, coarse, mine, pair, parts, send_sems, recv_sems):
+def combine(plan, grids, here, remote, gathers, levels, coefs, ly, lz, planes, out, coarse, mine, pair, parts):
     members, rows = plan.members, plan.rows
-    here = lax.axis_index("space")
-    grid = lax.axis_index("grid")
-    partner = grid + 1 - 2 * lax.rem(grid, 2)
-    space_peers = [{"space": lax.rem(here + d, members)} for d in range(1, members)]
-    grid_peers = [{"grid": partner}] + [{"grid": lax.rem(grid + 2 * d, grids)} for d in range(1, grids // 2)]
-    peers = space_peers + grid_peers
-
-    barrier = pltpu.get_barrier_semaphore()
-    for peer in peers:
-        pl.semaphore_signal(barrier, inc=1, device_id=peer, device_id_type=pl.DeviceIdType.MESH)
-    pl.semaphore_wait(barrier, len(peers))
-
-    def remote(source, target, number):
-        return pltpu.make_async_remote_copy(
-            src_ref=source,
-            dst_ref=target,
-            send_sem=send_sems.at[number],
-            recv_sem=recv_sems.at[number],
-            device_id=peers[number],
-            device_id_type=pl.DeviceIdType.MESH,
-        )
-
-    gathers = [remote(planes.at[0], coarse.at[here], i) for i in range(members - 1)]
-    for copy in gathers:
-        copy.start()
-    coarse[here] = planes[0]
-
     mask = grid_mask(levels, ly, lz)
     weight = coefs[0].astype(jnp.float32)
     fine = {}
@@ -342,6 +147,7 @@
         fine[k] = planes[k] - 0.5 * planes[k - h]
         if k + h < rows:
             fine[k] = fine[k] - 0.5 * planes[k + h]
+    coarse[here] = planes[0]
     for copy in gathers:
         copy.wait_recv()
     surplus = []
@@ -385,6 +191,203 @@
         copy.wait_send()
 
 
+def surplus_kernel(
+    plan, grids, slab, groups, chunk, levels, coefs, ly, lz, dens, kap, hy, hz, out,
+    raw_d, raw_k, dprev, kprev, dnext, knext, f_a, f_b, fx, fy, fz, planes, coarse, mine, pair, parts,
+    sems, halo_send, halo_recv, send_sems, recv_sems,
+):
+    halo = ITERS
+    chunks = slab // chunk
+    copies = []
+    for c in range(chunks):
+        part = pl.ds(c * chunk, chunk)
+        both_copies = (
+            pltpu.make_async_copy(kap.at[0, part], raw_k.at[part], sems.at[0, c]),
+            pltpu.make_async_copy(dens.at[0, part], raw_d.at[part], sems.at[1, c]),
+        )
+        for copy in both_copies:
+            copy.start()
+        copies.append(both_copies)
+
+    here = lax.axis_index("space")
+    up = {"space": lax.rem(here + 1, plan.members)}
+    down = {"space": lax.rem(here + plan.members - 1, plan.members)}
+    grid = lax.axis_index("grid")
+    partner = grid + 1 - 2 * lax.rem(grid, 2)
+    peers = [{"space": lax.rem(here + d, plan.members)} for d in range(1, plan.members)]
+    peers += [{"grid": partner}] + [{"grid": lax.rem(grid + 2 * d, grids)} for d in range(1, grids // 2)]
+    barrier = pltpu.get_barrier_semaphore()
+    for peer in peers:
+        pl.semaphore_signal(barrier, inc=1, device_id=peer, device_id_type=pl.DeviceIdType.MESH)
+    pl.semaphore_wait(barrier, len(peers))
+
+    def remote(source, target, number):
+        return pltpu.make_async_remote_copy(
+            src_ref=source,
+            dst_ref=target,
+            send_sem=send_sems.at[number],
+            recv_sem=recv_sems.at[number],
+            device_id=peers[number],
+            device_id_type=pl.DeviceIdType.MESH,
+        )
+
+    last, initial = pl.ds(slab - halo, halo), pl.ds(0, 1)
+    sends = []
+    for i, (source, target, peer) in enumerate(
+        (
+            (kap.at[0, last], kprev, up),
+            (dens.at[0, last], dprev, up),
+            (kap.at[0, initial], knext, down),
+            (dens.at[0, initial], dnext, down),
+        )
+    ):
+        copy = pltpu.make_async_remote_copy(
+            src_ref=source,
+            dst_ref=target,
+            send_sem=halo_send.at[i],
+            recv_sem=halo_recv.at[i],
+            device_id=peer,
+            device_id_type=pl.DeviceIdType.MESH,
+        )
+        copy.start()
+        sends.append(copy)
+
+    def natural(ref, row):
+        return jnp.stack([ref[row, pl.ds(j, 8, stride=groups), :] for j in range(groups)], axis=0)
+
+    def first(r, k_above, d_above, carry):
+        k, d, flux = carry
+        x_face = 0.5 * (k + k_above)
+        y_face = 0.5 * (k + next_y(k))
+        z_face = 0.5 * (k + next_lane(k))
+        fx[r - 1] = x_face
+        fy[r - 1] = y_face
+        fz[r - 1] = z_face
+        f_a[r - 1], flux = row_update(d, d_above, flux, x_face, y_face, z_face)
+        return k_above, d_above, flux
+
+    def both(x, carry):
+        return first(x + halo, natural(raw_k, x), natural(raw_d, x), carry)
+
+    zero = jnp.zeros((groups, 8, LANES), jnp.float32)
+    for c in range(chunks):
+        for copy in copies[c]:
+            copy.wait()
+        start, rest = c * chunk, chunk
+        if c == 0:
+            carry = (natural(raw_k, 0), natural(raw_d, 0), zero)
+            start, rest = 1, chunk - 1
+
+        def several(i, carry, start=start):
+            for u in range(UNROLL):
+                carry = both(start + i * UNROLL + u, carry)
+            return carry
+
+        carry = lax.fori_loop(0, rest // UNROLL, several, carry)
+        for x in range(start + rest // UNROLL * UNROLL, start + rest):
+            carry = both(x, carry)
+    for copy in sends:
+        copy.wait_recv()
+    first(slab + halo, natural(knext, 0), natural(dnext, 0), carry)
+    carry = (natural(kprev, 0), natural(dprev, 0), zero)
+    for r in range(1, halo):
+        carry = first(r, natural(kprev, r), natural(dprev, r), carry)
+    carry = both(0, carry)
+    f_a[halo] = f_a[halo] - carry[2]
+
+    stride = plan.stride
+    left = ITERS - 2
+    old, new_f = f_a, f_b
+    while 2 * left + 1 >= stride:
+        low, high = halo - left, halo + slab - stride + left
+        count, rest = (high - low + 1) // UNROLL, (high - low + 1) % UNROLL
+
+        def one(r, carry, old=old, new_f=new_f):
+            row, flux = carry
+            above = old[r + 1]
+            new_f[r], flux = row_update(row, above, flux, fx[r], fy[r], fz[r])
+            return above, flux
+
+        def several_steps(i, carry, low=low, one=one):
+            for u in range(UNROLL):
+                carry = one(low + UNROLL * i + u, carry)
+            return carry
+
+        row = old[low]
+        flux = fx[low - 1] * (row - old[low - 1])
+        carry = lax.fori_loop(0, count, several_steps, (row, flux))
+        for r in range(low + UNROLL * count, high + 1):
+            carry = one(r, carry)
+        old, new_f = new_f, old
+        left -= 1
+
+    def cone_step(center, wanted, reach, old, new_f):
+        def near(j, far):
+            return any(min((j - w) % groups, (w - j) % groups) <= far for w in wanted)
+
+        flux = {}
+        for offset in range(-reach, reach + 1):
+            need = [j for j in range(groups) if near(j, reach - abs(offset))]
+            r = center + offset
+            cells = {}
+
+            def cell(j):
+                if j not in cells:
+                    cells[j] = old[r, j]
+                return cells[j]
+
+            below, flux, fluxes_y = flux, {}, {}
+
+            def flux_y(j):
+                if j not in fluxes_y:
+                    follow = cell(j + 1) if j + 1 < groups else pltpu.roll(cell(0), 7, 0)
+                    fluxes_y[j] = fy[r, j] * (follow - cell(j))
+                return fluxes_y[j]
+
+            for j in need:
+                here = cell(j)
+                flux[j] = fx[r, j] * (old[r + 1, j] - here)
+                lower = below[j] if j in below else fx[r - 1, j] * (here - old[r - 1, j])
+                before = flux_y(j - 1) if j else pltpu.roll(flux_y(groups - 1), 1, 0)
+                gz = fz[r, j] * (next_lane(here) - here)
+                new_f[r, j] = ((here + flux[j]) + (flux_y(j) + gz)) - ((lower + before) + last_lane(gz))
+
+    period = min(8, plan.rows)
+
+    def cones(i, _):
+        source, target = old, new_f
+        for reach in range(left, -1, -1):
+            for k in range(period):
+                spare = EXTRA if k == 0 else min(EXTRA, trailing_zeros(k))
+                step = max(1, groups >> spare)
+                center = halo + (i * period + k) * stride
+                cone_step(center, list(range(0, groups, step)), reach, source, target)
+            source, target = target, source
+        return 0
+
+    done = old if left % 2 else new_f
+
+    def transform(k_low, k_high):
+        part = [done[halo + k * stride].reshape(groups * 8, LANES) for k in range(k_low, k_high)]
+        part = split_dot(jnp.concatenate(part, axis=0), hz[...], False)
+        size, count = groups * 8, k_high - k_low
+        part = jnp.concatenate([part[i * size : (i + 1) * size] for i in range(count)], axis=1)
+        part = split_dot(hy[...], part, True)
+        for i in range(count):
+            planes[k_low + i] = part[:, i * LANES : (i + 1) * LANES]
+
+    cones(0, 0)
+    transform(0, 1)
+    gathers = [remote(planes.at[0], coarse.at[here], i) for i in range(plan.members - 1)]
+    for copy in gathers:
+        copy.start()
+    lax.fori_loop(1, plan.rows // period, cones, 0)
+    transform(1, plan.rows)
+    combine(plan, grids, here, remote, gathers, levels, coefs, ly, lz, planes, out, coarse, mine, pair, parts)
+    for copy in sends:
+        copy.wait_send()
+
+
 def expand_kernel(plan, slab, pos_ref, levels, ly, lz, dy, dz, packed, out, coarse, nodes, buf, sems):
     mask = grid_mask(levels, ly, lz)
     members, rows, stride = plan.members, plan.rows, plan.stride
@@ -470,37 +473,31 @@
     raw = pltpu.VMEM((slab, width_y, width_z), jnp.float32)
     below = pltpu.VMEM((ITERS, width_y, width_z), jnp.float32)
     above = pltpu.VMEM((1, width_y, width_z), jnp.float32)
-    planes = pl.pallas_call(
-        functools.partial(diffuse_kernel, plan, slab, groups, chunk),
-        out_shape=jax.ShapeDtypeStruct((plan.rows, kept, LANES), jnp.float32),
-        in_specs=[anywhere, anywhere, vmem, vmem],
-        out_specs=vmem,
-        scratch_shapes=[raw, raw, below, below, above, above]
-        + [extended] * 5
-        + [pltpu.SemaphoreType.DMA((2, slab // chunk)), pltpu.SemaphoreType.DMA((4,)), pltpu.SemaphoreType.DMA((4,))],
-        compiler_params=pltpu.CompilerParams(vmem_limit_bytes=VMEM_LIMIT, collective_id=1, has_side_effects=True),
-        name="diffuse",
-    )(density, kappa, hy, hz)
-
     grids = lax.axis_size("grid")
     peers = members - 1 + grids // 2
     packed_shape = (plan.tiles, 8, LANES)
     packed = pl.pallas_call(
-        functools.partial(combine_kernel, plan, grids),
+        functools.partial(surplus_kernel, plan, grids, slab, groups, chunk),
         out_shape=jax.ShapeDtypeStruct(packed_shape, jnp.float32),
-        in_specs=[smem, smem] + [vmem] * 3,
+        in_specs=[smem, smem, vmem, vmem, anywhere, anywhere, vmem, vmem],
         out_specs=vmem,
-        scratch_shapes=[
+        scratch_shapes=[raw, raw, below, below, above, above]
+        + [extended] * 5
+        + [
+            pltpu.VMEM((plan.rows, kept, LANES), jnp.float32),
             pltpu.VMEM((members, kept, LANES), jnp.float32),
             pltpu.VMEM(packed_shape, jnp.float32),
             pltpu.VMEM(packed_shape, jnp.float32),
             pltpu.VMEM((grids // 2,) + packed_shape, jnp.float32),
+            pltpu.SemaphoreType.DMA((2, slab // chunk)),
+            pltpu.SemaphoreType.DMA((4,)),
+            pltpu.SemaphoreType.DMA((4,)),
             pltpu.SemaphoreType.DMA((peers,)),
             pltpu.SemaphoreType.DMA((peers,)),
         ],
         compiler_params=pltpu.CompilerParams(vmem_limit_bytes=VMEM_LIMIT, collective_id=0, has_side_effects=True),
-        name="combine",
-    )(levels, coefs, ly, lz, planes)
+        name="surplus",
+    )(levels, coefs, ly, lz, density, kappa, hy, hz)
 
     return pl.pallas_call(
         functools.partial(expand_kernel, plan, slab),

time: 50.7 us -> 55.3 us (1.091)
  Pallas kernels: 49.7 us -> 54.4 us
    pallas_call x2 -> x1, Pallas kernels: 46.1 us -> 50.8 us  [local(): pl.pallas_call(functools.partial(surplus_kernel, plan, grids, slab, group...]
where the time goes in v5:
time: 55.3 us; the launch traced here: 55 us
  Pallas kernels  54.4 us (98%)
  between operations  0.66 us (1%)
    pallas_call x1, Pallas kernels, local(): pl.pallas_call(functools.partial(surplus_kernel, plan, grids, slab, group...  50.8 us
    pallas_call x1, Pallas kernels, local(): pl.pallas_call(functools.partial(expand_kernel, plan, slab), out_shape=ja...  3.62 us

profile of v5, /device:TPU:0, one launch (start us, length us, event | category | flops | bytes accessed | tf_op | source)
XLA Modules:
  0.0 55.0 jit_solution(5866223888662227198)
XLA Ops:
  0.7 50.8 %surplus.1.packed = f32[9,8,128]{2,1,0:T(8,128)} custom-call(s32[1,3]{1,0:T(1,128)} %levels.3, s32[1]{0:T(128)S(6)} %copy.11.coefs, s32[64,128]{1,0:T(8,128)} %constant.20.clone.ly, s32[64,128]{1,0:T(8,128)} %constant.21.clone.lz, f32[1,128,64,128]{3,2,1,0:T(8,128)} %dens.1, f32[1,128,64,128]{3,2,1,0:T(8,128)} %kap.1, bf16[64,64]{1,0:T(8,128)(2,1)} %constant.16.clone.hy, ...), custom_call_target="tpu_custom_call" | custom-call | tf_op jit(solution)/shard_map/surplus/pallas_call | solution.py:479
  51.4 3.6 %expand.1 = f32[1,128,64,128]{3,2,1,0:T(8,128)} custom-call(s32[1]{0:T(128)} %bitcast.pos_ref, s32[1,3]{1,0:T(1,128)} %levels.3, s32[64,128]{1,0:T(8,128)} %constant.20.clone.ly, s32[64,128]{1,0:T(8,128)} %constant.21.clone.lz, bf16[64,64]{1,0:T(8,128)(2,1)} %constant.18.clone.dy, bf16[128,128]{1,0:T(8,128)(2,1)} %constant.19.clone.dz, ...), custom_call_target="tpu_custom_call" | custom-call | tf_op jit(solution)/shard_map/expand/pallas_call | solution.py:502
